TPU v7x, 32 devices: a whole 2x2x4 slice. The times are simulated.
32 devices in a mesh: group: 4 (over y, core), dev: 8 (over z, x).
Axes of the slice: x: 2, y: 2, z: 4, core: 2. Of those that a mesh axis runs over, the one named last changes fastest.
Arguments:
- node_state: bfloat16 [16384, 512], P(('group', 'dev')), may hold values from -6 to 6
- hub_state: bfloat16 [64, 512], P('dev'), may hold values from -6 to 6
- w_edge_in: bfloat16 [512, 256], replicated, may hold values from -0.25 to 0.25
- w_edge_out: bfloat16 [256, 512], replicated, may hold values from -0.375 to 0.375
- w_update: bfloat16 [512, 512], replicated, may hold values from -0.25 to 0.25
- edge_src: int32 [131072], P(('group', 'dev')), may hold values from 0 to 319
- edge_dst: int32 [131072], P(('group', 'dev')), may hold values from 0 to 319
- edge_mask: int32 [131072], P(('group', 'dev')), may hold values 0 or 1
- send_list: int32 [32, 8, 32], P(('group', 'dev')), may hold values from 0 to 511
- send_count: int32 [32, 8], P(('group', 'dev')), may hold values from 8 to 32, as said below
- node_cot: bfloat16 [16384, 512], P(('group', 'dev')), may hold values from -0.059814453 to 0.059814453
- hub_cot: bfloat16 [64, 512], P('dev'), may hold values from -0.059814453 to 0.059814453
Outputs:
- new_state: bfloat16 [16384, 512], P(('group', 'dev'))
- new_hub: bfloat16 [64, 512], P('dev')
- grad_in: float32 [512, 256], replicated
- grad_out: float32 [256, 512], replicated
- grad_update: float32 [512, 512], replicated
Inputs may be any that keep to these rules, and one draw needn't show every extreme that they name: Device 0 sends 32 live slots to peer 0: send_count[0, 0] = 32.
All inputs are finite; a program needn't handle non-finite values. No bound on the sum of `edge_mask` on one device may be relied on, other than what follows from the above.
Results may differ from a plain program's by a relative error of at most 0.0064.
The roundings to bfloat16 on the way count: a program that leaves them out, or rounds other values in their place, can miss the bound.
Values may be sent and summed in bfloat16 or wider, within the bound.
No kernel may reach another device: no remote copies, remote signals or barrier semaphores. Data moves between devices by JAX's collectives and lax.ppermute only.
A program may use at most 64 MiB of HBM per device.

v0:
```python
import jax
import jax.numpy as jnp
from jax import lax
from jax.sharding import PartitionSpec as P


def silu_grad(values):
    sigmoid_v = jax.nn.sigmoid(values)
    return sigmoid_v * (1.0 + values * (1.0 - sigmoid_v))


def finish(states, summed, degree, w_update):
    mean_part = summed / jnp.maximum(degree, 1.0)[:, None]
    mixed_rows = (states.astype(jnp.float32) + mean_part).astype(jnp.bfloat16)
    pre_update = jnp.dot(mixed_rows, w_update, preferred_element_type=jnp.float32)
    updated = (states.astype(jnp.float32) + jax.nn.silu(pre_update)).astype(jnp.bfloat16)
    return (mixed_rows, pre_update, updated)


def backward_rows(cotangent, pre_update, degree, w_update):
    grad_pre = (cotangent.astype(jnp.float32) * silu_grad(pre_update)).astype(jnp.bfloat16)
    grad_mix = jnp.dot(grad_pre, w_update.T, preferred_element_type=jnp.float32)
    grad_sum = (grad_mix / jnp.maximum(degree, 1.0)[:, None]).astype(jnp.bfloat16)
    return (grad_pre, grad_sum)


def shards(
    node_state,
    hub_state,
    w_edge_in,
    w_edge_out,
    w_update,
    edge_src,
    edge_dst,
    edge_mask,
    send_list,
    send_count,
    node_cot,
    hub_cot,
):
    width = node_state.shape[1]
    master_rows = node_state.shape[0]
    send_rows = send_list[0]
    peer_total = send_rows.shape[0]
    slot_width = send_rows.shape[1]
    mirror_total = peer_total * slot_width
    live_slot = jnp.arange(slot_width)[None, :] < send_count[0][:, None]
    flat_rows = send_rows.reshape(-1)
    flat_live = live_slot.reshape(-1)
    selector = (
        (flat_rows[:, None] == jnp.arange(master_rows)[None, :]) & flat_live[:, None]
    ).astype(jnp.bfloat16)
    contract = (((0,), (0,)), ((), ()))
    outgoing = jnp.dot(selector, node_state, preferred_element_type=jnp.float32).astype(
        jnp.bfloat16
    )
    mirror_rows = lax.all_to_all(
        outgoing.reshape(peer_total, slot_width, width),
        "dev",
        split_axis=0,
        concat_axis=0,
        tiled=True,
    )
    hub_table = lax.all_gather(hub_state, "dev", axis=0, tiled=True)
    local_table = jnp.concatenate([mirror_rows.reshape(mirror_total, width), hub_table], axis=0)
    local_rows = local_table.shape[0]
    edge_total = edge_src.shape[0]
    block_size = min(1024, edge_total)
    block_count = edge_total // block_size
    sources = edge_src.reshape(block_count, block_size)
    targets = edge_dst.reshape(block_count, block_size)
    edge_keep = edge_mask.reshape(block_count, block_size)
    row_ids = jnp.arange(local_rows)[None, :]

    def forward_step(totals, pieces):
        source_ids, target_ids, keep_ids = pieces
        gathered = local_table[source_ids]
        pre_act = jnp.dot(gathered, w_edge_in, preferred_element_type=jnp.float32)
        hidden = jax.nn.silu(pre_act).astype(jnp.bfloat16)
        message = jnp.dot(hidden, w_edge_out, preferred_element_type=jnp.float32).astype(
            jnp.bfloat16
        )
        onehot = ((target_ids[:, None] == row_ids) & (keep_ids[:, None] > 0)).astype(jnp.bfloat16)
        added = lax.dot_general(onehot, message, contract, preferred_element_type=jnp.float32)
        tally = jnp.sum(onehot, axis=0, dtype=jnp.float32)
        return ((totals[0] + added, totals[1] + tally), pre_act)

    start_fwd = (jnp.zeros((local_rows, width), jnp.float32), jnp.zeros((local_rows,), jnp.float32))
    (partial_value, counts_local), saved_acts = lax.scan(
        forward_step, start_fwd, (sources, targets, edge_keep)
    )
    mirror_part = (
        partial_value[:mirror_total].reshape(peer_total, slot_width, width).astype(jnp.bfloat16)
    )
    mirror_count = counts_local[:mirror_total].reshape(peer_total, slot_width).astype(jnp.bfloat16)
    back_part, back_count = (
        lax.all_to_all(mirror_part, "dev", split_axis=0, concat_axis=0, tiled=True),
        lax.all_to_all(mirror_count, "dev", split_axis=0, concat_axis=0, tiled=True),
    )
    summed = lax.dot_general(
        selector,
        back_part.reshape(mirror_total, width),
        contract,
        preferred_element_type=jnp.float32,
    )
    degree = lax.dot_general(
        selector, back_count.reshape(mirror_total, 1), contract, preferred_element_type=jnp.float32
    )[:, 0]
    hub_part = partial_value[mirror_total:]
    hub_count = counts_local[mirror_total:]
    whole_part, whole_count = (
        lax.psum(hub_part.astype(jnp.bfloat16), "group").astype(jnp.float32),
        lax.psum(hub_count.astype(jnp.bfloat16), "group").astype(jnp.float32),
    )
    hub_summed, hub_degree = (
        lax.psum_scatter(
            whole_part.astype(jnp.bfloat16), "dev", scatter_dimension=0, tiled=True
        ).astype(jnp.float32),
        lax.psum_scatter(
            whole_count.astype(jnp.bfloat16), "dev", scatter_dimension=0, tiled=True
        ).astype(jnp.float32),
    )
    mixed_rows, pre_update, new_state = finish(node_state, summed, degree, w_update)
    hub_mixed, hub_pre, new_hub = finish(hub_state, hub_summed, hub_degree, w_update)
    grad_pre, grad_sum = backward_rows(node_cot, pre_update, degree, w_update)
    hub_grad_pre, hub_grad_sum = backward_rows(hub_cot, hub_pre, hub_degree, w_update)
    grad_outgoing = jnp.dot(selector, grad_sum, preferred_element_type=jnp.float32).astype(
        jnp.bfloat16
    )
    grad_mirror = lax.all_to_all(
        grad_outgoing.reshape(peer_total, slot_width, width),
        "dev",
        split_axis=0,
        concat_axis=0,
        tiled=True,
    )
    grad_hubs = lax.all_gather(hub_grad_sum, "dev", axis=0, tiled=True)
    grad_table = jnp.concatenate([grad_mirror.reshape(mirror_total, width), grad_hubs], axis=0)
    hub_weight = (lax.axis_index("group") == 0).astype(jnp.float32)
    grad_update = lax.dot_general(
        mixed_rows, grad_pre, contract, preferred_element_type=jnp.float32
    )
    grad_update = grad_update + hub_weight * lax.dot_general(
        hub_mixed, hub_grad_pre, contract, preferred_element_type=jnp.float32
    )

    def backward_step(totals, pieces):
        source_ids, target_ids, keep_ids, pre_act = pieces
        gathered = local_table[source_ids]
        hidden = jax.nn.silu(pre_act).astype(jnp.bfloat16)
        grad_message = jnp.where(
            keep_ids[:, None] > 0, grad_table[target_ids], jnp.zeros((), jnp.bfloat16)
        )
        grad_w_out = lax.dot_general(
            hidden, grad_message, contract, preferred_element_type=jnp.float32
        )
        grad_hidden = jnp.dot(grad_message, w_edge_out.T, preferred_element_type=jnp.float32)
        grad_act = (grad_hidden * silu_grad(pre_act)).astype(jnp.bfloat16)
        grad_w_in = lax.dot_general(
            gathered, grad_act, contract, preferred_element_type=jnp.float32
        )
        return ((totals[0] + grad_w_in, totals[1] + grad_w_out), None)

    start = (jnp.zeros(w_edge_in.shape, jnp.float32), jnp.zeros(w_edge_out.shape, jnp.float32))
    local_grads, _ = lax.scan(backward_step, start, (sources, targets, edge_keep, saved_acts))
    grad_in, grad_out, grad_upd = lax.psum(
        (local_grads[0], local_grads[1], grad_update), ("group", "dev")
    )
    return (new_state, new_hub, grad_in, grad_out, grad_upd)


def solution(mesh):
    return jax.shard_map(
        shards,
        mesh=mesh,
        in_specs=(
            P(("group", "dev"), None),
            P("dev", None),
            P(),
            P(),
            P(),
            P(("group", "dev")),
            P(("group", "dev")),
            P(("group", "dev")),
            P(("group", "dev"), None, None),
            P(("group", "dev"), None),
            P(("group", "dev"), None),
            P("dev", None),
        ),
        out_specs=(P(("group", "dev"), None), P("dev", None), P(), P(), P()),
        check_vma=False,
    )
```

profile of v0, /device:TPU:0, one launch (start us, length us, event | category | flops | bytes accessed | tf_op | source)
XLA Modules:
  0.0 417.0 jit_solution(8544541724577750692)
XLA Ops:
  10.9 7.2 %all-to-all-start = ((bf16[8,32,512]{2,1,0:T(8,128)(2,1)}), bf16[8,32,512]{2,1,0:T(8,128)(2,1)S(1)}, u32[]{:S(2)}, u32[]{:S(2)}) async-start(bf16[8,32,512]{2,1,0:T(8,128)(2,1)} %bitcast.1), calls=%async_computation | async-start | bytes 524288 | tf_op jit(solution)/shard_map/all_to_all | solution.py:57
  20.4 31.2 %all_gather.6 = bf16[64,512]{1,0:T(8,128)(2,1)S(1)} all-gather(bf16[8,512]{1,0:T(8,128)(2,1)} %param.17), channel_id=1, replica_groups=mesh['group'=4,'dev'=8] {'dev'}, dimensions={0}, use_global_device_ids=true | all-gather | bytes 73728 | tf_op jit(solution)/shard_map/all_gather | solution.py:64
  51.7 33.4 %while.28 = (s32[]{:T(128)}, f32[320,512]{1,0:T(8,128)}, f32[320]{0:T(512)S(1)}, f32[4,1024,256]{2,1,0:T(8,128)}, s32[4,1024]{1,0:T(4,128)S(1)}, /*index=5*/s32[...) while((s32[]{:T(128)}, f32[320,512]{1,0:T(8,128)}, ...), condition=%wide.region_2.3_spmd.clone, body=%wide.region_0.2_spmd.clone.sunk | while | flops 876877120 | bytes 10273476 | solution.py:89
  51.8 4.0 gather_fusion
  59.3 4.0 gather_fusion
  67.9 4.0 gather_fusion
  76.5 4.0 gather_fusion
  85.8 5.4 %all-to-all-start.2 = ((bf16[8,1,32]{2,1,0:T(2,128)(2,1)}), bf16[8,1,32]{2,1,0:T(2,128)(2,1)S(1)}, u32[]{:S(2)}, u32[]{:S(2)}) async-start(bf16[8,1,32]{2,1,0:T(2,128)(2,1)} %convert_element_type.118), calls=%async_computation.2 | async-start | bytes 8192 | tf_op jit(solution)/shard_map/all_to_all | solution.py:98
  95.1 21.8 %all-reduce = bf16[64]{0:T(256)(128)(2,1)S(1)} all-reduce(bf16[64]{0:T(256)(128)(2,1)S(1)} %slice.27), channel_id=3, replica_groups=mesh['group'=4,'dev'=8] {'dev'}, use_global_device_ids=true, to_apply=%region_6.7.clone | all-reduce | flops 64 | bytes 256
  120.8 38.2 %reduce-scatter.2.cloned.1.call-done = bf16[8,512]{1,0:T(8,128)(2,1)} async-done(((bf16[64,512]{1,0:T(8,128)(2,1)}), bf16[8,512]{1,0:T(8,128)(2,1)}) %reduce-scatter.2.cloned.1.call-update) | async-done | bytes 8208 | tf_op jit(solution)/shard_map/reduce_scatter | solution.py:116
  159.0 6.0 %all-reduce.2 = (bf16[8,512]{1,0:T(8,128)(2,1)S(1)}, bf16[8]{0:T(256)(128)(2,1)S(1)}) all-reduce(bf16[8,512]{1,0:T(8,128)(2,1)} %reduce-scatter.2.cloned.1.call-done, bf16[8]{0:T(256)(128)(2,1)S(1)} %dynamic-slice.1), channel_id=1, replica_groups=mesh['group'=4,'dev'=8] {'group'}, use_global_device_ids=true, to_apply=%region_3.4 | all-reduce | flops 4104 | bytes 16416 | tf_op jit(solution)/shard_map/psum | solution.py:112
  166.1 30.5 %all_gather.7 = bf16[64,512]{1,0:T(8,128)(2,1)S(1)} all-gather(bf16[8,512]{1,0:T(8,128)(2,1)S(1)} %fusion.42), channel_id=1, replica_groups=mesh['group'=4,'dev'=8] {'dev'}, dimensions={0}, use_global_device_ids=true | all-gather | bytes 73728 | tf_op jit(solution)/shard_map/all_gather | solution.py:137
  202.3 3.6 all-to-all-start.3
  207.8 6.3 %all-to-all-done.3 = bf16[8,32,512]{2,1,0:T(8,128)(2,1)S(1)} async-done(((bf16[8,32,512]{2,1,0:T(8,128)(2,1)}), bf16[8,32,512]{2,1,0:T(8,128)(2,1)S(1)}, u32[]{:S(2)}, u32[]{:S(2)}) %all-to-all-start.3) | async-done | bytes 262176 | tf_op jit(solution)/shard_map/all_to_all | solution.py:130
  214.1 56.7 %while.29 = (s32[]{:T(128)}, f32[512,256]{1,0:T(8,128)}, f32[256,512]{1,0:T(8,128)}, s32[4,1024]{1,0:T(4,128)S(1)}, bf16[320,512]{1,0:T(8,128)(2,1)S(1)}, /*inde...) while((s32[]{:T(128)}, f32[512,256]{1,0:T(8,128)}, ...), condition=%wide.region_8.9_spmd.clone, body=%wide.region_7.8_spmd.clone.sunk | while | flops 810558464 | bytes 11845768 | solution.py:165
  214.2 4.0 gather_fusion.2
  218.2 4.0 gather_fusion.1
  228.1 4.0 gather_fusion.2
  232.1 4.0 gather_fusion.1
  242.4 4.0 gather_fusion.2
  246.3 4.0 gather_fusion.1
  256.6 4.0 gather_fusion.2
  260.6 4.0 gather_fusion.1
  270.8 133.3 %all-reduce.5.cloned.1.call-done = (f32[512,256]{1,0:T(8,128)}, f32[256,512]{1,0:T(8,128)}, f32[512,512]{1,0:T(8,128)}) async-done(((f32[512,256]{1,0:T(8,128)}, f32[256,512]{1,0:T(8,128)}, f32[512,512]{1,0:T(8,128)}), (f32[512,256]{1,0:T(8,128)}, f32[256,512]{1,0:T(8,128)}, f32[512,512]{1,0:T(8,128)})) %all-reduce.5.cloned.1.call-update) | async-done | bytes 2097168 | tf_op jit(solution)/shard_map/psum | solution.py:166
  (128 shorter events, 70.4 us)
Async XLA Ops:
  7.2 157.8 %copy-start = (bf16[512,512]{1,0:T(8,128)(2,1)S(1)}, bf16[512,512]{1,0:T(8,128)(2,1)}, u32[]{:S(2)}) copy-start(bf16[512,512]{1,0:T(8,128)(2,1)} %param.20) | copy-start | bytes 1572868
  10.9 40.7 %all-to-all-start = ((bf16[8,32,512]{2,1,0:T(8,128)(2,1)}), bf16[8,32,512]{2,1,0:T(8,128)(2,1)S(1)}, u32[]{:S(2)}, u32[]{:S(2)}) async-start(bf16[8,32,512]{2,1,0:T(8,128)(2,1)} %bitcast.1), calls=%async_computation | async-start | bytes 524288 | tf_op jit(solution)/shard_map/all_to_all | solution.py:57
  51.7 39.6 %copy-start.6 = (u32[32]{0:T(128)S(1)}, u32[32]{0:T(128)}, u32[]{:S(2)}) copy-start(u32[32]{0:T(128)} %constant.65) | copy-start | bytes 388
  51.7 113.3 %copy-start.2 = (bf16[8,512]{1,0:T(8,128)(2,1)S(1)}, bf16[8,512]{1,0:T(8,128)(2,1)}, u32[]{:S(2)}) copy-start(bf16[8,512]{1,0:T(8,128)(2,1)} %param.17) | copy-start | bytes 24580
  51.7 114.2 %copy-start.3 = (bf16[8,512]{1,0:T(8,128)(2,1)S(1)}, bf16[8,512]{1,0:T(8,128)(2,1)}, u32[]{:S(2)}) copy-start(bf16[8,512]{1,0:T(8,128)(2,1)} %param.27) | copy-start | bytes 24580
  51.7 4.0 copy-start.1
  51.8 5.5 %copy-start.5 = (bf16[256,512]{1,0:T(8,128)(2,1)S(1)}, bf16[256,512]{1,0:T(8,128)(2,1)}, u32[]{:S(2)}) copy-start(bf16[256,512]{1,0:T(8,128)(2,1)} %get-tuple-element.406) | copy-start | bytes 786436 | tf_op jit(solution)/shard_map/while
  59.2 4.0 copy-start.1
  59.3 5.5 %copy-start.5 = (bf16[256,512]{1,0:T(8,128)(2,1)S(1)}, bf16[256,512]{1,0:T(8,128)(2,1)}, u32[]{:S(2)}) copy-start(bf16[256,512]{1,0:T(8,128)(2,1)} %get-tuple-element.406) | copy-start | bytes 786436 | tf_op jit(solution)/shard_map/while
  67.9 4.0 copy-start.1
  67.9 5.5 %copy-start.5 = (bf16[256,512]{1,0:T(8,128)(2,1)S(1)}, bf16[256,512]{1,0:T(8,128)(2,1)}, u32[]{:S(2)}) copy-start(bf16[256,512]{1,0:T(8,128)(2,1)} %get-tuple-element.406) | copy-start | bytes 786436 | tf_op jit(solution)/shard_map/while
  76.5 4.0 copy-start.1
  76.5 5.5 %copy-start.5 = (bf16[256,512]{1,0:T(8,128)(2,1)S(1)}, bf16[256,512]{1,0:T(8,128)(2,1)}, u32[]{:S(2)}) copy-start(bf16[256,512]{1,0:T(8,128)(2,1)} %get-tuple-element.406) | copy-start | bytes 786436 | tf_op jit(solution)/shard_map/while
  85.8 31.2 %all-to-all-start.2 = ((bf16[8,1,32]{2,1,0:T(2,128)(2,1)}), bf16[8,1,32]{2,1,0:T(2,128)(2,1)S(1)}, u32[]{:S(2)}, u32[]{:S(2)}) async-start(bf16[8,1,32]{2,1,0:T(2,128)(2,1)} %convert_element_type.118), calls=%async_computation.2 | async-start | bytes 8192 | tf_op jit(solution)/shard_map/all_to_all | solution.py:98
  91.2 67.8 %reduce-scatter.2.cloned.1.call-start = ((), (), s32[]{:S(2)}) async-start(), calls=%async_computation.5 | async-start | bytes 73728 | tf_op jit(solution)/shard_map/reduce_scatter | solution.py:116
  92.5 105.6 %copy-start.4 = (bf16[512,512]{1,0:T(8,128)(2,1)S(1)}, bf16[512,512]{1,0:T(8,128)(2,1)}, u32[]{:S(2)}) copy-start(bf16[512,512]{1,0:T(8,128)(2,1)} %param.26) | copy-start | bytes 1572868
  117.0 79.6 %all-to-all-start.1 = ((bf16[8,32,512]{2,1,0:T(8,128)(2,1)}), bf16[8,32,512]{2,1,0:T(8,128)(2,1)S(1)}, u32[]{:S(2)}, u32[]{:S(2)}) async-start(bf16[8,32,512]{2,1,0:T(8,128)(2,1)} %bitcast.3), calls=%async_computation.1 | async-start | bytes 524288 | tf_op jit(solution)/shard_map/all_to_all | solution.py:97
  202.3 11.8 %all-to-all-start.3 = ((bf16[8,32,512]{2,1,0:T(8,128)(2,1)}), bf16[8,32,512]{2,1,0:T(8,128)(2,1)S(1)}, u32[]{:S(2)}, u32[]{:S(2)}) async-start(bf16[8,32,512]{2,1,0:T(8,128)(2,1)} %bitcast.6), calls=%async_computation.3 | async-start | bytes 524288 | tf_op jit(solution)/shard_map/all_to_all | solution.py:130
  205.9 198.3 %all-reduce.5.cloned.1.call-start = ((), (), s32[]{:S(2)}) async-start(), calls=%async_computation.6 | async-start | bytes 4194304 | tf_op jit(solution)/shard_map/psum | solution.py:166
Sparse Core Ops, SparseCore 0:
  96.0 62.9 reduce-scatter.1
  270.9 133.1 all-reduce.4
where the time goes:
time: 418 us; the launch traced here: 417 us
  waiting for transfers between devices  178 us (43%)
  blocking collectives  89.5 us (21%)
  local copies, waits for them, and re-layouts  59.5 us (14%)
  matrix products  51.1 us (12%)
  starting transfers between devices  19.8 us (5%)
  between operations  14.9 us (4%)
    psum x1, waiting for transfers between devices, shards(): lax.psum((local_grads[0], local_grads[1], grad_update), ('group', 'dev'))  133 us
    reduce_scatter x1, waiting for transfers between devices, shards(): lax.psum_scatter(whole_part.astype(jnp.bfloat16), 'dev', scatter_dimensio...  38.2 us
    all_gather x1, blocking collectives, shards(): hub_table = lax.all_gather(hub_state, 'dev', axis=0, tiled=True)  31.2 us
    all_gather x1, blocking collectives, shards(): grad_hubs = lax.all_gather(hub_grad_sum, 'dev', axis=0, tiled=True)  30.5 us
    unnamed x1, blocking collectives  21.8 us
    gather x4, local copies, waits for them, and re-layouts, backward_step(): grad_table[target_ids]  15.9 us
    gather x4, local copies, waits for them, and re-layouts, forward_step(): gathered = local_table[source_ids]  15.9 us
    gather x4, local copies, waits for them, and re-layouts, backward_step(): gathered = local_table[source_ids]  15.9 us
  transfers between devices with their start and end apart: 6, of which 3 were waited for; matrix products, arithmetic and copies ran while one was open for 2% of the time, Pallas kernels for 0%

commit v1 on v0

v1 whole, which is shorter than its diff:
```python
import jax
import jax.numpy as jnp
from jax import lax
from jax.sharding import PartitionSpec as P

F32 = jnp.float32
BF16 = jnp.bfloat16


def silu_grad(values):
    sigmoid_v = jax.nn.sigmoid(values)
    return sigmoid_v * (1.0 + values * (1.0 - sigmoid_v))


def dot(left, right, dims=((1,), (0,))):
    return lax.dot_general(left, right, (dims, ((), ())), preferred_element_type=F32)


def split_dot(left, right, dims):
    high = left.astype(BF16)
    low = (left - high.astype(F32)).astype(BF16)
    return dot(high, right, dims) + dot(low, right, dims)


def swap(blocks, axis, size, stride, total):
    position = lax.rem(lax.div(lax.axis_index(axis), stride), size)
    if size == 2:
        pairs = [(i, i ^ stride) for i in range(total)]
        other = lax.ppermute(lax.dynamic_index_in_dim(blocks, 1 - position, 0, False), axis, pairs)
        own = lax.dynamic_index_in_dim(blocks, position, 0, False)
        first = position == 0
        return jnp.stack([jnp.where(first, own, other), jnp.where(first, other, own)])
    if size * stride == total and stride == 1:
        groups = None
    else:
        groups = [
            [base + off + i * stride for i in range(size)]
            for base in range(0, total, size * stride)
            for off in range(stride)
        ]
    return lax.all_to_all(blocks, axis, 0, 0, tiled=True, axis_index_groups=groups)


def scatter_sum(value, axis, size, stride, total):
    position = lax.rem(lax.div(lax.axis_index(axis), stride), size)
    blocks = value.reshape(size, -1, value.shape[1])
    if size == 2:
        pairs = [(i, i ^ stride) for i in range(total)]
        sent = lax.dynamic_index_in_dim(blocks, 1 - position, 0, False).astype(BF16)
        own = lax.dynamic_index_in_dim(blocks, position, 0, False)
        return own + lax.ppermute(sent, axis, pairs).astype(F32)
    return jnp.sum(swap(blocks.astype(BF16), axis, size, stride, total).astype(F32), axis=0)


def gather_all(value, axis, size, stride, total):
    spread = jnp.broadcast_to(value[None], (size,) + value.shape)
    return swap(spread, axis, size, stride, total).reshape(-1, value.shape[1])


def shards(
    node_state,
    hub_state,
    w_edge_in,
    w_edge_out,
    w_update,
    edge_src,
    edge_dst,
    edge_mask,
    send_list,
    send_count,
    node_cot,
    hub_cot,
    *,
    n_group,
    n_dev,
):
    width = node_state.shape[1]
    hidden_width = w_edge_in.shape[1]
    master_rows = node_state.shape[0]
    send_rows = send_list[0]
    slot_width = send_rows.shape[1]
    mirror_total = n_dev * slot_width
    hub_rows = hub_state.shape[0]
    live_slot = jnp.arange(slot_width)[None, :] < send_count[0][:, None]
    chosen = jnp.where(live_slot, send_rows, -1).reshape(1, -1)
    select = (jnp.arange(master_rows)[:, None] == chosen).astype(BF16)

    outgoing = dot(select, node_state, ((0,), (0,))).astype(BF16)
    packed = jnp.concatenate(
        [
            outgoing.reshape(n_dev, slot_width, width),
            jnp.broadcast_to(hub_state[None], (n_dev, hub_rows, width)),
        ],
        axis=1,
    )
    arrived = lax.all_to_all(packed, "dev", 0, 0, tiled=True)
    table = jnp.concatenate(
        [
            arrived[:, :slot_width].reshape(mirror_total, width),
            arrived[:, slot_width:].reshape(-1, width),
        ],
        axis=0,
    )
    local_rows = table.shape[0]

    ids = jnp.arange(local_rows)[:, None]
    from_hot = (ids == edge_src[None, :]).astype(BF16)
    to_hot = (ids == jnp.where(edge_mask > 0, edge_dst, -1)[None, :]).astype(BF16)
    adjacency = dot(to_hot, from_hot, ((1,), (1,)))
    adj_high = jnp.floor(adjacency * (1.0 / 256.0))
    adj_low = (adjacency - 256.0 * adj_high).astype(BF16)
    adj_high = adj_high.astype(BF16)
    counts = jnp.sum(adjacency, axis=1)

    pre_act = dot(table, w_edge_in)
    hidden = jax.nn.silu(pre_act).astype(BF16)
    partial = dot(adj_low, hidden) + 256.0 * dot(adj_high, hidden)

    def by_peer(value, hubs_of):
        return jnp.concatenate(
            [
                value[:mirror_total].reshape((n_dev, slot_width) + value.shape[1:]),
                value[mirror_total:].reshape((n_dev, hubs_of) + value.shape[1:]),
            ],
            axis=1,
        )

    rounded_count = counts.astype(BF16)
    rest_count = (counts - rounded_count.astype(F32)).astype(BF16)
    count_rows = jnp.stack([by_peer(rounded_count, hub_rows), by_peer(rest_count, hub_rows)], axis=1)
    count_rows = jnp.pad(
        count_rows, ((0, 0), (0, 6), (0, hidden_width - slot_width - hub_rows))
    )
    message = jnp.concatenate([by_peer(partial.astype(BF16), hub_rows), count_rows], axis=1)
    back = lax.all_to_all(message, "dev", 0, 0, tiled=True)
    base = slot_width + hub_rows
    back_part = back[:, :slot_width].reshape(mirror_total, hidden_width)
    back_count = back[:, base, :slot_width].reshape(mirror_total, 1)
    summed_hidden = dot(select, back_part)
    degree = dot(select, back_count)
    hub_hidden = jnp.sum(back[:, slot_width:base].astype(F32), axis=0)
    hub_degree = jnp.sum(back[:, base : base + 2, slot_width:base].astype(F32), axis=(0, 1))
    hub_sums = jnp.concatenate(
        [hub_hidden, jnp.broadcast_to(hub_degree[:, None], (hub_rows, 128))], axis=1
    )
    hub_sums = lax.psum(hub_sums, "group")
    hub_hidden, hub_degree = hub_sums[:, :hidden_width], hub_sums[:, hidden_width : hidden_width + 1]

    states = jnp.concatenate([node_state, hub_state], axis=0).astype(F32)
    cotangent = jnp.concatenate([node_cot, hub_cot], axis=0).astype(F32)
    degree = jnp.maximum(jnp.concatenate([degree, hub_degree], axis=0), 1.0)
    summed_hidden = jnp.concatenate([summed_hidden, hub_hidden], axis=0)
    summed = split_dot(summed_hidden, w_edge_out, ((1,), (0,)))
    mixed = (states + summed / degree).astype(BF16)
    pre_update = dot(mixed, w_update)
    updated = (states + jax.nn.silu(pre_update)).astype(BF16)
    grad_pre = (cotangent * silu_grad(pre_update)).astype(BF16)
    grad_sum = (dot(grad_pre, w_update, ((1,), (1,))) / degree).astype(BF16)
    grad_hidden = dot(grad_sum, w_edge_out, ((1,), (1,))).astype(BF16)

    grad_outgoing = dot(select, grad_hidden[:master_rows], ((0,), (0,))).astype(BF16)
    packed_grad = jnp.concatenate(
        [
            grad_outgoing.reshape(n_dev, slot_width, hidden_width),
            jnp.broadcast_to(grad_hidden[None, master_rows:], (n_dev, hub_rows, hidden_width)),
        ],
        axis=1,
    )
    arrived_grad = lax.all_to_all(packed_grad, "dev", 0, 0, tiled=True)
    grad_rows = jnp.concatenate(
        [
            arrived_grad[:, :slot_width].reshape(mirror_total, hidden_width),
            arrived_grad[:, slot_width:].reshape(-1, hidden_width),
        ],
        axis=0,
    )

    row_weight = jnp.where(
        jnp.arange(mixed.shape[0])[:, None] < master_rows,
        1.0,
        (lax.axis_index("group") == 0).astype(F32),
    )
    weighted = (grad_pre.astype(F32) * row_weight).astype(BF16)
    grad_update = dot(mixed, weighted, ((0,), (0,)))
    grad_out = split_dot(summed_hidden * row_weight, grad_sum, ((0,), (0,)))

    by_source = dot(adj_low, grad_rows, ((0,), (0,))) + 256.0 * dot(
        adj_high, grad_rows, ((0,), (0,))
    )
    grad_act = by_source * silu_grad(pre_act)
    act_high = grad_act.astype(BF16)
    act_low = (grad_act - act_high.astype(F32)).astype(BF16)
    grad_in = dot(table, act_high, ((0,), (0,))) + dot(table, act_low, ((0,), (0,)))

    half = width // 2
    side = jnp.concatenate([grad_in[:half], grad_in[half:]], axis=1)
    whole = jnp.concatenate([grad_update, grad_out, side], axis=0)
    whole = scatter_sum(whole, "group", 2, 1, n_group)
    whole = scatter_sum(whole, "group", n_group // 2, 2, n_group)
    whole = scatter_sum(whole, "dev", n_dev, 1, n_dev)
    whole = gather_all(whole.astype(BF16), "dev", n_dev, 1, n_dev)
    whole = gather_all(whole, "group", n_group // 2, 2, n_group)
    whole = gather_all(whole, "group", 2, 1, n_group).astype(F32)
    side = whole[width + hidden_width :]
    return (
        updated[:master_rows],
        updated[master_rows:],
        jnp.concatenate([side[:, :hidden_width], side[:, hidden_width:]], axis=0),
        whole[width : width + hidden_width],
        whole[:width],
    )


def solution(mesh):
    def body(*args):
        return shards(*args, n_group=mesh.shape["group"], n_dev=mesh.shape["dev"])

    return jax.shard_map(
        body,
        mesh=mesh,
        in_specs=(
            P(("group", "dev"), None),
            P("dev", None),
            P(),
            P(),
            P(),
            P(("group", "dev")),
            P(("group", "dev")),
            P(("group", "dev")),
            P(("group", "dev"), None, None),
            P(("group", "dev"), None),
            P(("group", "dev"), None),
            P("dev", None),
        ),
        out_specs=(P(("group", "dev"), None), P("dev", None), P(), P(), P()),
        check_vma=False,
    )
```

time: 418 us -> 115 us (0.28)
  waiting for transfers between devices: 178 us -> 33.9 us
  blocking collectives: 89.5 us -> 33.1 us
  local copies, waits for them, and re-layouts: 59.5 us -> 9.5 us
  matrix products: 51.1 us -> 12.1 us
  between operations: 14.9 us -> 1.15 us
    psum x1 -> x0, waiting for transfers between devices: 133 us -> none  [shards(): lax.psum((local_grads[0], local_grads[1], grad_update), ('group', 'dev'))]
    all_gather x2 -> x0, blocking collectives: 61.7 us -> none  [the longest x1 31.2 us: shards(): hub_table = lax.all_gather(hub_state, 'dev', axis=0, tiled=True)]
    gather x12 -> x0, local copies, waits for them, and re-layouts: 47.6 us -> none  [the longest x4 15.9 us: backward_step(): grad_table[target_ids]]
    dot_general x25 -> x20, matrix products: 51.1 us -> 12.1 us  [dot(): lax.dot_general(left, right, (dims, ((), ())), preferred_element_type=F32)]
    reduce_scatter x1 -> x0, waiting for transfers between devices: 38.2 us -> none  [shards(): lax.psum_scatter(whole_part.astype(jnp.bfloat16), 'dev', scatter_dimensio...]
    all_to_all x0 -> x2, blocking collectives: none -> 23 us  [swap(): lax.all_to_all(blocks, axis, 0, 0, tiled=True, axis_index_groups=groups)]
    unnamed x1 -> x0, blocking collectives: 21.8 us -> none
    ppermute x0 -> x4, waiting for transfers between devices: none -> 14.1 us  [the longest x2 8.81 us: scatter_sum(): return own + lax.ppermute(sent, axis, pairs).astype(F32)]
  transfers between devices with their start and end apart: 6 -> 7, of which waited for: 3 -> 7; matrix products, arithmetic and copies ran while one was open for 2% -> 6% of each run, Pallas kernels for 0% -> 0%
where the time goes in v1:
time: 115 us; the launch traced here: 114 us
  waiting for transfers between devices  33.9 us (29%)
  blocking collectives  33.1 us (29%)
  starting transfers between devices  17.5 us (15%)
  matrix products  12.1 us (11%)
  local copies, waits for them, and re-layouts  9.5 us (8%)
  other arithmetic  6.87 us (6%)
    all_to_all x2, blocking collectives, swap(): lax.all_to_all(blocks, axis, 0, 0, tiled=True, axis_index_groups=groups)  23 us
    dot_general x20, matrix products, dot(): lax.dot_general(left, right, (dims, ((), ())), preferred_element_type=F32)  12.1 us
    psum x1, blocking collectives, shards(): hub_sums = lax.psum(hub_sums, 'group')  10.1 us
    ppermute x2, waiting for transfers between devices, scatter_sum(): return own + lax.ppermute(sent, axis, pairs).astype(F32)  8.81 us
    all_to_all x1, waiting for transfers between devices, shards(): arrived = lax.all_to_all(packed, 'dev', 0, 0, tiled=True)  7.98 us
    all_to_all x1, waiting for transfers between devices, shards(): back = lax.all_to_all(message, 'dev', 0, 0, tiled=True)  7.78 us
    all_to_all x1, starting transfers between devices, shards(): arrived = lax.all_to_all(packed, 'dev', 0, 0, tiled=True)  7.25 us
    ppermute x2, waiting for transfers between devices, swap(): lax.ppermute(lax.dynamic_index_in_dim(blocks, 1 - position, 0, False), ax...  5.28 us
  transfers between devices with their start and end apart: 7, of which 7 were waited for; matrix products, arithmetic and copies ran while one was open for 6% of the time, Pallas kernels for 0%

profile of v1, /device:TPU:0, one launch (start us, length us, event | category | flops | bytes accessed | tf_op | source)
XLA Modules:
  0.0 114.2 jit_solution(3356900994865378915)
XLA Ops:
  2.3 1.4 %convolution_convert_fusion.1 = bf16[256,512]{1,0:T(8,128)(2,1)S(1)} fusion(bf16[512,512]{1,0:T(8,128)(2,1)} %param.12, s32[256]{0:T(256)S(1)} %broadcast_select_fusion), kind=kOutput, calls=%fused_computation.16 | convolution fusion | flops 134479872 | bytes 787456 | tf_op jit(solution)/shard_map/dot_general | solution.py:16
  5.2 7.3 %all-to-all-start = ((bf16[8,40,512]{2,1,0:T(8,128)(2,1)}), bf16[8,40,512]{2,1,0:T(8,128)(2,1)S(1)}, u32[]{:S(2)}, u32[]{:S(2)}) async-start(bf16[8,40,512]{2,1,0:T(8,128)(2,1)} %pad_maximum_fusion.4), calls=%async_computation | async-start | bytes 655360 | tf_op jit(solution)/shard_map/all_to_all | solution.py:96
  12.5 2.0 %fusion.62 = (f32[320]{0:T(512)S(1)}, f32[320,320]{0,1:T(8,128)S(1)}) fusion(s32[4096]{0:T(1024)S(1)} %copy-done.13, s32[4096]{0:T(1024)S(1)} %compare_select_fusion), kind=kOutput, calls=%fused_computation.120 | convolution fusion | flops 841584320 | bytes 443648 | tf_op jit(solution)/shard_map/dot_general | solution.py:16
  14.8 8.0 %all-to-all-done = bf16[8,40,512]{2,1,0:T(8,128)(2,1)S(1)} async-done(((bf16[8,40,512]{2,1,0:T(8,128)(2,1)}), bf16[8,40,512]{2,1,0:T(8,128)(2,1)S(1)}, u32[]{:S(2)}, u32[]{:S(2)}) %all-to-all-start) | async-done | bytes 327712 | tf_op jit(solution)/shard_map/all_to_all | solution.py:96
  24.5 3.6 %all-to-all-start.1 = ((bf16[8,48,256]{2,1,0:T(8,128)(2,1)}), bf16[8,48,256]{2,1,0:T(8,128)(2,1)S(1)}, u32[]{:S(2)}, u32[]{:S(2)}) async-start(bf16[8,48,256]{2,1,0:T(8,128)(2,1)} %fusion.33), calls=%async_computation.1 | async-start | bytes 393216 | tf_op jit(solution)/shard_map/all_to_all | solution.py:135
  28.1 7.8 %all-to-all-done.1 = bf16[8,48,256]{2,1,0:T(8,128)(2,1)S(1)} async-done(((bf16[8,48,256]{2,1,0:T(8,128)(2,1)}), bf16[8,48,256]{2,1,0:T(8,128)(2,1)S(1)}, u32[]{:S(2)}, u32[]{:S(2)}) %all-to-all-start.1) | async-done | bytes 196640 | tf_op jit(solution)/shard_map/all_to_all | solution.py:135
  36.0 10.1 %psum.7 = f32[8,384]{1,0:T(8,128)S(1)} all-reduce(f32[8,384]{1,0:T(8,128)S(1)} %pad_maximum_fusion.16), channel_id=1, replica_groups=mesh['group'=4,'dev'=8] {'group'}, use_global_device_ids=true, to_apply=%region_3.4 | all-reduce | flops 3072 | bytes 24576 | tf_op jit(solution)/shard_map/psum | solution.py:146
  48.6 1.7 %multiply_convert_fusion.1 = (bf16[520,512]{1,0:T(8,128)(2,1)S(1)}, bf16[520,512]{1,0:T(8,128)(2,1)}) fusion(bf16[8,512]{1,0:T(8,128)(2,1)S(1)} %copy-done.14, bf16[512,512]{1,0:T(8,128)(2,1)S(1)} %copy-done.11, bf16[8,512]{1,0:T(8,128)(2,1)S(1)} %copy-done.10, bf16[512,512]{1,0:T(8,128)(2,1)S(1)} %copy-done.12, bf16[520,512]{1,0:T(8,128)(2,1)S(1)} %fusion.5, ...), kind=kOutput, calls=%fused_computation.26 | convolution fusion | flops 277954560 | bytes 3186688 | tf_op jit(solution)/shard_map/dot_general | solution.py:16
  52.5 3.4 %all-to-all-start.2 = ((bf16[8,40,256]{2,1,0:T(8,128)(2,1)}), bf16[8,40,256]{2,1,0:T(8,128)(2,1)S(1)}, u32[]{:S(2)}, u32[]{:S(2)}) async-start(bf16[8,40,256]{2,1,0:T(8,128)(2,1)} %pad_maximum_fusion.9), calls=%async_computation.2 | async-start | bytes 327680 | tf_op jit(solution)/shard_map/all_to_all | solution.py:169
  57.7 1.7 %fusion.12 = f32[512,512]{1,0:T(8,128)} fusion(bf16[520,512]{1,0:T(8,128)(2,1)S(1)} %copy-done.16, bf16[520,512]{1,0:T(8,128)(2,1)S(1)} %copy-done.18, f32[520]{0:T(1024)S(1)} %fusion.44), kind=kOutput, calls=%fused_computation.32 | convolution fusion | flops 273428480 | bytes 2115616 | tf_op jit(solution)/shard_map/dot_general | solution.py:16
  59.3 4.1 %all-to-all-done.2 = bf16[8,40,256]{2,1,0:T(8,128)(2,1)S(1)} async-done(((bf16[8,40,256]{2,1,0:T(8,128)(2,1)}), bf16[8,40,256]{2,1,0:T(8,128)(2,1)S(1)}, u32[]{:S(2)}, u32[]{:S(2)}) %all-to-all-start.2) | async-done | bytes 163872 | tf_op jit(solution)/shard_map/all_to_all | solution.py:169
  65.9 2.0 %collective-permute-done = bf16[512,512]{1,0:T(8,128)(2,1)} collective-permute-done((bf16[512,512]{1,0:T(8,128)(2,1)S(1)}, bf16[512,512]{1,0:T(8,128)(2,1)}, u32[]{:S(2)}, u32[]{:S(2)}) %collective-permute-start) | collective-permute-done | bytes 524320 | tf_op jit(solution)/shard_map/ppermute | solution.py:51
  67.9 1.2 %bitcast_add_fusion = f32[512,512]{1,0:T(8,128)S(1)} fusion(bf16[512,512]{1,0:T(8,128)(2,1)} %collective-permute-done, f32[2,512,512]{2,1,0:T(8,128)S(1)} %bitcast.66, s32[]{:T(128)S(6)} %select_n.70), kind=kLoop, calls=%fused_computation.30 | loop fusion | flops 524288 | bytes 2621444 | tf_op jit(solution)/shard_map/add | solution.py:51
  69.1 1.0 copy-done.1
  70.1 1.6 %collective-permute-start.1 = (bf16[256,512]{1,0:T(8,128)(2,1)S(1)}, bf16[256,512]{1,0:T(8,128)(2,1)S(1)}, u32[]{:S(2)}, u32[]{:S(2)}) collective-permute-start(bf16[256,512]{1,0:T(8,128)(2,1)S(1)} %fusion.23), channel_id=1, source_target_pairs={{0,16},{8,24},{16,0},{24,8},{1,17},{9,25},{17,1},{25,9},{2,18},{10... | collective-permute-start | bytes 786440 | tf_op jit(solution)/shard_map/ppermute | solution.py:51
  71.7 6.8 %collective-permute-done.1 = bf16[256,512]{1,0:T(8,128)(2,1)S(1)} collective-permute-done((bf16[256,512]{1,0:T(8,128)(2,1)S(1)}, bf16[256,512]{1,0:T(8,128)(2,1)S(1)}, u32[]{:S(2)}, u32[]{:S(2)}) %collective-permute-start.1) | collective-permute-done | bytes 262176 | tf_op jit(solution)/shard_map/ppermute | solution.py:51
  78.6 1.1 fusion.15
  79.7 11.1 %all_to_all.25 = bf16[8,32,512]{2,1,0:T(8,128)(2,1)S(1)} all-to-all(bf16[8,32,512]{2,1,0:T(8,128)(2,1)S(1)} %bitcast.74), channel_id=1, replica_groups=mesh['group'=4,'dev'=8] {'dev'}, dimensions={0} | all-to-all | bytes 524288 | tf_op jit(solution)/shard_map/all_to_all | solution.py:41
  90.8 11.9 %all_to_all.26 = bf16[8,32,512]{2,1,0:T(8,128)(2,1)S(1)} all-to-all(bf16[8,32,512]{2,1,0:T(8,128)(2,1)S(1)} %broadcast_in_dim.32), channel_id=1, replica_groups=mesh['group'=4,'dev'=8] {'dev'}, dimensions={0} | all-to-all | bytes 524288 | tf_op jit(solution)/shard_map/all_to_all | solution.py:41
  102.7 1.5 %collective-permute-start.2 = (bf16[256,512]{1,0:T(8,128)(2,1)S(1)}, bf16[256,512]{1,0:T(8,128)(2,1)S(1)}, u32[]{:S(2)}, u32[]{:S(2)}) collective-permute-start(bf16[256,512]{1,0:T(8,128)(2,1)S(1)} %bitcast.73), channel_id=1, source_target_pairs={{0,16},{8,24},{16,0},{24,8},{1,17},{9,25},{17,1},{25,9},{2,18},{10... | collective-permute-start | bytes 786440 | tf_op jit(solution)/shard_map/ppermute | solution.py:29
  104.3 4.8 %collective-permute-done.2 = bf16[256,512]{1,0:T(8,128)(2,1)S(1)} collective-permute-done((bf16[256,512]{1,0:T(8,128)(2,1)S(1)}, bf16[256,512]{1,0:T(8,128)(2,1)S(1)}, u32[]{:S(2)}, u32[]{:S(2)}) %collective-permute-start.2) | collective-permute-done | bytes 262176 | tf_op jit(solution)/shard_map/ppermute | solution.py:29
  109.3 0.8 slice.131
  111.5 0.8 slice.141
  112.3 1.0 slice_bitcast_fusion
  (108 shorter events, 16.4 us)
Async XLA Ops:
  0.6 47.3 %copy-start = (bf16[512,512]{1,0:T(8,128)(2,1)S(1)}, bf16[512,512]{1,0:T(8,128)(2,1)}, u32[]{:S(2)}) copy-start(bf16[512,512]{1,0:T(8,128)(2,1)} %param.16) | copy-start | bytes 1572868
  2.3 10.2 %copy-start.8 = (s32[4096]{0:T(1024)S(1)}, s32[4096]{0:T(1024)}, u32[]{:S(2)}) copy-start(s32[4096]{0:T(1024)} %param.18) | copy-start | bytes 49156
  2.3 10.2 %copy-start.9 = (s32[4096]{0:T(1024)S(1)}, s32[4096]{0:T(1024)}, u32[]{:S(2)}) copy-start(s32[4096]{0:T(1024)} %param.19) | copy-start | bytes 49156
  2.3 10.2 %copy-start.13 = (s32[4096]{0:T(1024)S(1)}, s32[4096]{0:T(1024)}, u32[]{:S(2)}) copy-start(s32[4096]{0:T(1024)} %param.17) | copy-start | bytes 49156
  5.2 17.6 %all-to-all-start = ((bf16[8,40,512]{2,1,0:T(8,128)(2,1)}), bf16[8,40,512]{2,1,0:T(8,128)(2,1)S(1)}, u32[]{:S(2)}, u32[]{:S(2)}) async-start(bf16[8,40,512]{2,1,0:T(8,128)(2,1)} %pad_maximum_fusion.4), calls=%async_computation | async-start | bytes 655360 | tf_op jit(solution)/shard_map/all_to_all | solution.py:96
  12.5 10.3 %copy-start.7 = (bf16[512,256]{1,0:T(8,128)(2,1)S(1)}, bf16[512,256]{1,0:T(8,128)(2,1)}, u32[]{:S(2)}) copy-start(bf16[512,256]{1,0:T(8,128)(2,1)} %param.14) | copy-start | bytes 786436
  14.5 8.9 %copy-start.5 = (f32[320,320]{0,1:T(8,128)}, f32[320,320]{0,1:T(8,128)S(1)}, u32[]{:S(2)}) copy-start(f32[320,320]{0,1:T(8,128)S(1)} %get-tuple-element.16) | copy-start | bytes 1228804
  23.8 23.1 %copy-start.2 = (bf16[256,512]{1,0:T(8,128)(2,1)S(1)}, bf16[256,512]{1,0:T(8,128)(2,1)}, u32[]{:S(2)}) copy-start(bf16[256,512]{1,0:T(8,128)(2,1)} %param.15) | copy-start | bytes 786436
  24.5 11.4 %all-to-all-start.1 = ((bf16[8,48,256]{2,1,0:T(8,128)(2,1)}), bf16[8,48,256]{2,1,0:T(8,128)(2,1)S(1)}, u32[]{:S(2)}, u32[]{:S(2)}) async-start(bf16[8,48,256]{2,1,0:T(8,128)(2,1)} %fusion.33), calls=%async_computation.1 | async-start | bytes 393216 | tf_op jit(solution)/shard_map/all_to_all | solution.py:135
  46.5 1.1 copy-start.12
  47.6 1.0 copy-start.11
  47.6 1.0 copy-start.14
  48.6 1.7 %copy-start.15 = (bf16[520,512]{1,0:T(8,128)(2,1)}, bf16[520,512]{1,0:T(8,128)(2,1)S(1)}, u32[]{:S(2)}) copy-start(bf16[520,512]{1,0:T(8,128)(2,1)S(1)} %fusion.5) | copy-start | bytes 1597444
  52.5 10.9 %all-to-all-start.2 = ((bf16[8,40,256]{2,1,0:T(8,128)(2,1)}), bf16[8,40,256]{2,1,0:T(8,128)(2,1)S(1)}, u32[]{:S(2)}, u32[]{:S(2)}) async-start(bf16[8,40,256]{2,1,0:T(8,128)(2,1)} %pad_maximum_fusion.9), calls=%async_computation.2 | async-start | bytes 327680 | tf_op jit(solution)/shard_map/all_to_all | solution.py:169
  56.5 1.1 copy-start.16
  56.5 1.2 %copy-start.18 = (bf16[520,512]{1,0:T(8,128)(2,1)S(1)}, bf16[520,512]{1,0:T(8,128)(2,1)}, u32[]{:S(2)}) copy-start(bf16[520,512]{1,0:T(8,128)(2,1)} %copy-done.17) | copy-start | bytes 1597444
  57.7 5.8 %copy-start.6 = (f32[320,320]{0,1:T(8,128)S(1)}, f32[320,320]{0,1:T(8,128)}, u32[]{:S(2)}) copy-start(f32[320,320]{0,1:T(8,128)} %copy-done.5) | copy-start | bytes 1228804
  64.3 1.2 %copy-start.3 = (f32[512,512]{1,0:T(8,128)S(1)}, f32[512,512]{1,0:T(8,128)}, u32[]{:S(2)}) copy-start(f32[512,512]{1,0:T(8,128)} %fusion.12) | copy-start | bytes 3145732
  65.8 2.1 %collective-permute-start = (bf16[512,512]{1,0:T(8,128)(2,1)S(1)}, bf16[512,512]{1,0:T(8,128)(2,1)}, u32[]{:S(2)}, u32[]{:S(2)}) collective-permute-start(bf16[512,512]{1,0:T(8,128)(2,1)S(1)} %fusion.14), channel_id=1, source_target_pairs={{0,8},{8,0},{16,24},{24,16},{1,9},{9,1},{17,25},{25,17},{2,10},{10... | collective-permute-start | bytes 1572872 | tf_op jit(solution)/shard_map/ppermute | solution.py:51
  69.1 1.0 copy-start.1
  70.1 8.4 %collective-permute-start.1 = (bf16[256,512]{1,0:T(8,128)(2,1)S(1)}, bf16[256,512]{1,0:T(8,128)(2,1)S(1)}, u32[]{:S(2)}, u32[]{:S(2)}) collective-permute-start(bf16[256,512]{1,0:T(8,128)(2,1)S(1)} %fusion.23), channel_id=1, source_target_pairs={{0,16},{8,24},{16,0},{24,8},{1,17},{9,25},{17,1},{25,9},{2,18},{10... | collective-permute-start | bytes 786440 | tf_op jit(solution)/shard_map/ppermute | solution.py:51
  102.7 6.6 %copy-start.4 = (bf16[520,512]{1,0:T(8,128)(2,1)S(1)}, bf16[520,512]{1,0:T(8,128)(2,1)}, u32[]{:S(2)}) copy-start(bf16[520,512]{1,0:T(8,128)(2,1)} %get-tuple-element.8) | copy-start | bytes 1597444
  102.7 6.4 %collective-permute-start.2 = (bf16[256,512]{1,0:T(8,128)(2,1)S(1)}, bf16[256,512]{1,0:T(8,128)(2,1)S(1)}, u32[]{:S(2)}, u32[]{:S(2)}) collective-permute-start(bf16[256,512]{1,0:T(8,128)(2,1)S(1)} %bitcast.73), channel_id=1, source_target_pairs={{0,16},{8,24},{16,0},{24,8},{1,17},{9,25},{17,1},{25,9},{2,18},{10... | collective-permute-start | bytes 786440 | tf_op jit(solution)/shard_map/ppermute | solution.py:29
  109.2 2.0 %collective-permute-start.3 = (bf16[512,512]{1,0:T(8,128)(2,1)S(1)}, bf16[512,512]{1,0:T(8,128)(2,1)S(1)}, u32[]{:S(2)}, u32[]{:S(2)}) collective-permute-start(bf16[512,512]{1,0:T(8,128)(2,1)S(1)} %bitcast.72), channel_id=1, source_target_pairs={{0,8},{8,0},{16,24},{24,16},{1,9},{9,1},{17,25},{25,17},{2,10},{10... | collective-permute-start | bytes 1572872 | tf_op jit(solution)/shard_map/ppermute | solution.py:29
  (2 other events, 1.5 us)

commit v2 on v0

v2 whole, which is shorter than its diff:
```python
import functools

import jax
import jax.numpy as jnp
from jax import lax
from jax.experimental import pallas as pl
from jax.experimental.pallas import tpu as pltpu
from jax.sharding import PartitionSpec as P

F32 = jnp.float32
BF16 = jnp.bfloat16
I32 = jnp.int32
NN = ((1,), (0,))
NT = ((1,), (1,))
TN = ((0,), (0,))


def dot(left, right, dims=NN):
    return lax.dot_general(left, right, (dims, ((), ())), preferred_element_type=F32)


def halves(value):
    high = value.astype(BF16)
    return high, (value - high.astype(F32)).astype(BF16)


def silu(values):
    return values * jax.nn.sigmoid(values)


def silu_grad(values):
    sigmoid_v = jax.nn.sigmoid(values)
    return sigmoid_v * (1.0 + values * (1.0 - sigmoid_v))


def iota(shape, axis):
    return lax.broadcasted_iota(I32, shape, axis)


class Layout:
    def __init__(self, peers, slots, hubs):
        self.peers, self.slots, self.hubs = peers, slots, hubs
        self.base = slots + hubs
        self.block = -(-(self.base + 2) // 16) * 16
        self.rows = peers * self.block

    def place(self, ids):
        mirrors = self.peers * self.slots
        slot_bits, hub_bits = self.slots.bit_length() - 1, self.hubs.bit_length() - 1
        hub_ids = ids - mirrors
        mirror_row = (ids >> slot_bits) * self.block + (ids & (self.slots - 1))
        hub_row = (hub_ids >> hub_bits) * self.block + self.slots + (hub_ids & (self.hubs - 1))
        return jnp.where(ids < mirrors, mirror_row, hub_row)


def gather_body(lay, chosen_ref, rows_ref, hubs_ref, out_ref):
    rows = rows_ref.shape[0]
    select = (iota((rows, lay.rows), 0) == chosen_ref[...]).astype(BF16)
    picked = dot(select, rows_ref[...], TN)
    hubs = hubs_ref[...].astype(F32)
    rest = jnp.zeros((lay.block - lay.base, hubs.shape[1]), F32)
    for peer in range(lay.peers):
        start = peer * lay.block
        part = [picked[start : start + lay.slots], hubs, rest]
        out_ref[start : start + lay.block, :] = jnp.concatenate(part, axis=0).astype(BF16)


def count_body(
    lay, src_ref, dst_ref, mask_ref, low_ref, high_ref, low_t_ref, high_t_ref, rows_ref, sum_ref
):
    steps, chunk = src_ref.shape
    ids = iota((lay.rows, chunk), 0)
    for step in range(steps):
        src = lay.place(src_ref[step : step + 1, :])
        keep = mask_ref[step : step + 1, :] > 0
        dst = jnp.where(keep, lay.place(dst_ref[step : step + 1, :]), -1)
        added = dot((ids == dst).astype(BF16), (ids == src).astype(BF16), NT)
        if step == 0:
            sum_ref[...] = added
        else:
            sum_ref[...] += added
    total = sum_ref[...]
    high = jnp.floor(total * (1.0 / 256.0))
    low = total - 256.0 * high
    low_ref[...] = low.astype(BF16)
    high_ref[...] = high.astype(BF16)
    low_t_ref[...] = low.T.astype(BF16)
    high_t_ref[...] = high.T.astype(BF16)
    counts = jnp.sum(total.T, axis=0, keepdims=True)
    rounded = counts.astype(BF16).astype(F32)
    shape = (lay.rows, lay.rows)
    row, col = iota(shape, 0), iota(shape, 1)
    row_block = jnp.floor((row.astype(F32) + 0.5) * (1.0 / lay.block))
    col_block = jnp.floor((col.astype(F32) + 0.5) * (1.0 / lay.block))
    row_rest = row.astype(F32) - lay.block * row_block
    same = row_block == col_block
    spread = jnp.where(same & (row_rest == lay.base), rounded, 0.0)
    spread += jnp.where(same & (row_rest == lay.base + 1), counts - rounded, 0.0)
    shape = (lay.rows, rows_ref.shape[1])
    row = iota(shape, 0).astype(F32)
    row_rest = row - lay.block * jnp.floor((row + 0.5) * (1.0 / lay.block))
    fold = (row_rest == iota(shape, 1).astype(F32)).astype(BF16)
    rows_ref[...] = dot(spread.astype(BF16), fold).astype(BF16)


def forward_body(table_ref, w_ref, low_ref, high_ref, rows_ref, out_ref):
    hidden = silu(dot(table_ref[...], w_ref[...])).astype(BF16)
    partial = dot(low_ref[...], hidden) + 256.0 * dot(high_ref[...], hidden)
    out_ref[...] = (partial + rows_ref[...].astype(F32)).astype(BF16)


def slope_body(n_group, n_dev, table_ref, w_ref, slope_ref, table_t_ref):
    slope_ref[...] = silu_grad(dot(table_ref[...], w_ref[...]))
    width = table_ref.shape[1]
    depth = width // (n_group * n_dev)
    depth_bits, dev_bits = depth.bit_length() - 1, n_dev.bit_length() - 1
    row = iota((width, width), 0)
    block = row >> depth_bits
    group, dev = block >> dev_bits, block & (n_dev - 1)
    order = (group & 1) * (n_group // 2) + (group >> 1)
    order = (order * 2 + (dev & 1)) * (n_dev // 2) + (dev >> 1)
    source = order * depth + (row & (depth - 1))
    turn = (iota((width, width), 1) == source).astype(BF16)
    table_t_ref[...] = dot(turn, table_ref[...], NT).astype(BF16)


def hub_sum_body(lay, back_ref, out_ref):
    width = back_ref.shape[1]
    hidden = jnp.zeros((lay.hubs, width), F32)
    counts = jnp.zeros((lay.block - lay.base, width), F32)
    for peer in range(lay.peers):
        start = peer * lay.block
        part = back_ref[start + lay.slots : start + lay.block, :].astype(F32)
        hidden += part[: lay.hubs]
        counts += part[lay.hubs :]
    count = counts[0:1] + counts[1:2]
    shape = (lay.hubs, width)
    own = iota(shape, 1) == iota(shape, 0) + lay.slots
    degree = jnp.sum(jnp.where(own, count, 0.0), axis=1, keepdims=True)
    out_ref[:, :width] = hidden
    out_ref[:, width:] = jnp.broadcast_to(degree, (lay.hubs, out_ref.shape[1] - width))


def update_rows(states, cotangent, hidden_sum, degree, w_out, w_update):
    high, low = halves(hidden_sum)
    share = 1.0 / jnp.maximum(degree, 1.0)
    mixed = (states + (dot(high, w_out) + dot(low, w_out)) * share).astype(BF16)
    pre = dot(mixed, w_update)
    updated = (states + silu(pre)).astype(BF16)
    grad_pre = (cotangent * silu_grad(pre)).astype(BF16)
    grad_sum = (dot(grad_pre, w_update, NT) * share).astype(BF16)
    grad_hidden = dot(grad_sum, w_out, NT).astype(BF16)
    return updated, mixed, grad_pre, high, low, grad_sum, grad_hidden


def master_body(
    lay,
    chosen_ref,
    back_ref,
    state_ref,
    cot_ref,
    w_out_ref,
    w_up_ref,
    new_ref,
    mixed_ref,
    pre_ref,
    high_ref,
    low_ref,
    sum_ref,
    out_ref,
):
    width = back_ref.shape[1]
    select = (iota((state_ref.shape[0], lay.rows), 0) == chosen_ref[...]).astype(BF16)
    back = back_ref[...]
    shape = (lay.rows, lay.rows)
    row, col = iota(shape, 0).astype(F32), iota(shape, 1).astype(F32)
    row_block = jnp.floor((row + 0.5) * (1.0 / lay.block))
    taken = (col == row_block * lay.block + lay.base).astype(BF16)
    shape = (lay.rows, width)
    row = iota(shape, 0).astype(F32)
    row_rest = row - lay.block * jnp.floor((row + 0.5) * (1.0 / lay.block))
    counts = jnp.where(row_rest == iota(shape, 1).astype(F32), dot(taken, back), 0.0)
    degree = jnp.sum(dot(select, counts.astype(BF16)), axis=1, keepdims=True)
    results = update_rows(
        state_ref[...].astype(F32),
        cot_ref[...].astype(F32),
        dot(select, back),
        degree,
        w_out_ref[...],
        w_up_ref[...],
    )
    updated, mixed, grad_pre, high, low, grad_sum, grad_hidden = results
    new_ref[...] = updated
    mixed_ref[...] = mixed
    pre_ref[...] = grad_pre
    high_ref[...] = high
    low_ref[...] = low
    sum_ref[...] = grad_sum
    out_ref[...] = dot(select, grad_hidden, TN)


def hub_body(
    lay,
    n_parts,
    *refs,
):
    parts = refs[:n_parts]
    state_ref, cot_ref, w_out_ref, w_up_ref, rows_ref = refs[n_parts : n_parts + 5]
    new_ref, mixed_ref, pre_ref, high_ref, low_ref, sum_ref, out_ref = refs[n_parts + 5 :]
    total = parts[0][...]
    for part in parts[1:]:
        total += part[...]
    width = rows_ref.shape[1]
    results = update_rows(
        state_ref[...].astype(F32),
        cot_ref[...].astype(F32),
        total[:, :width],
        total[:, width : width + 1],
        w_out_ref[...],
        w_up_ref[...],
    )
    updated, mixed, grad_pre, high, low, grad_sum, grad_hidden = results
    new_ref[...] = updated
    mixed_ref[...] = mixed
    pre_ref[...] = grad_pre
    high_ref[...] = high
    low_ref[...] = low
    sum_ref[...] = grad_sum
    hubs = grad_hidden.astype(F32)
    rest = jnp.zeros((lay.block - lay.base, width), F32)
    for peer in range(lay.peers):
        start = peer * lay.block
        part = [rows_ref[start : start + lay.slots, :], hubs, rest]
        out_ref[start : start + lay.block, :] = jnp.concatenate(part, axis=0).astype(BF16)


def weight_body(
    weight_ref,
    mixed_ref,
    pre_ref,
    high_ref,
    low_ref,
    sum_ref,
    hub_mixed_ref,
    hub_pre_ref,
    hub_high_ref,
    hub_low_ref,
    hub_sum_ref,
    out_ref,
):
    weight = weight_ref[0].astype(F32)
    rows = mixed_ref.shape[1]
    grad_sum, hub_grad = sum_ref[...], hub_sum_ref[...]
    out_ref[:rows, :] = dot(mixed_ref[...], pre_ref[...], TN) + weight * dot(
        hub_mixed_ref[...], hub_pre_ref[...], TN
    )
    hub_part = dot(hub_high_ref[...], hub_grad, TN) + dot(hub_low_ref[...], hub_grad, TN)
    main = dot(high_ref[...], grad_sum, TN) + dot(low_ref[...], grad_sum, TN)
    out_ref[rows:, :] = main + weight * hub_part


def backward_body(grad_ref, low_ref, high_ref, slope_ref, table_t_ref, out_ref):
    grad = grad_ref[...]
    by_source = dot(low_ref[...], grad) + 256.0 * dot(high_ref[...], grad)
    high, low = halves(by_source * slope_ref[...])
    table_t = table_t_ref[...]
    out_ref[...] = (dot(table_t, high) + dot(table_t, low)).astype(BF16)


def call(body, outs, args, scratch=(), flops=0, smem=0):
    outs = [jax.ShapeDtypeStruct(shape, kind) for shape, kind in outs]
    moved = sum(a.size * a.dtype.itemsize for a in list(args) + outs)
    vmem = pl.BlockSpec(memory_space=pltpu.VMEM)
    specs = [pl.BlockSpec(memory_space=pltpu.SMEM)] * smem + [vmem] * (len(args) - smem)
    single = len(outs) == 1
    return pl.pallas_call(
        body,
        out_shape=outs[0] if single else outs,
        in_specs=specs,
        out_specs=vmem if single else [vmem] * len(outs),
        scratch_shapes=list(scratch),
        compiler_params=pltpu.CompilerParams(vmem_limit_bytes=VMEM_LIMIT),
        cost_estimate=pl.CostEstimate(
            flops=int(flops), bytes_accessed=int(moved), transcendentals=0
        ),
    )(*args)


VMEM_LIMIT = 44 * 1024 * 1024


class Cube:
    def __init__(self, n_group, n_dev, parts):
        self.total = n_group * n_dev
        self.size, self.steps, self.place = 1, [0], 0
        for axis, stride, size in parts:
            unit = stride * (n_dev if axis == "group" else 1)
            place = lax.rem(lax.div(lax.axis_index(axis), stride), size)
            self.place = self.place * size + place
            self.steps = [s | (i * unit) for s in self.steps for i in range(size)]
            self.size *= size

    def send(self, value, step):
        pairs = [(i, i ^ self.steps[step]) for i in range(self.total)]
        return lax.ppermute(value, ("group", "dev"), pairs)

    def scatter(self, value):
        blocks = value.reshape(self.size, -1, value.shape[1])
        own = lax.dynamic_index_in_dim(blocks, self.place, 0, False)
        terms = []
        for step in range(1, self.size):
            block = lax.dynamic_index_in_dim(blocks, self.place ^ step, 0, False)
            terms.append(self.send(block.astype(BF16), step))
        return own, terms

    def gather(self, value):
        parts = [value] + [self.send(value, step) for step in range(1, self.size)]
        bit = 1
        while bit < self.size:
            flip = (self.place & bit) > 0
            parts = [jnp.where(flip, parts[i ^ bit], parts[i]) for i in range(self.size)]
            bit *= 2
        return jnp.concatenate(parts, axis=0)


def total(own, terms):
    for term in terms:
        own += term.astype(F32)
    return own


def shards(
    node_state,
    hub_state,
    w_edge_in,
    w_edge_out,
    w_update,
    edge_src,
    edge_dst,
    edge_mask,
    send_list,
    send_count,
    node_cot,
    hub_cot,
    *,
    n_group,
    n_dev,
):
    rows, width = node_state.shape
    hid = w_edge_in.shape[1]
    slots = send_list.shape[2]
    hubs = hub_state.shape[0]
    lay = Layout(n_dev, slots, hubs)
    both = ("group", "dev")
    live = jnp.arange(slots)[None, :] < send_count[0][:, None]
    chosen = jnp.where(live, send_list[0], -1)
    chosen = jnp.pad(chosen, ((0, 0), (0, lay.block - slots)), constant_values=-1).reshape(1, -1)

    def body(function, *static):
        return functools.partial(function, *static)

    packed = call(
        body(gather_body, lay), [((lay.rows, width), BF16)], [chosen, node_state, hub_state]
    )
    table = lax.all_to_all(packed, "dev", 0, 0, tiled=True)

    chunk = min(512, edge_src.shape[0])
    square = ((lay.rows, lay.rows), BF16)
    edges = [a.reshape(-1, chunk) for a in (edge_src, edge_dst, edge_mask)]
    low, high, low_t, high_t, count_rows = call(
        body(count_body, lay),
        [square, square, square, square, ((lay.rows, hid), BF16)],
        edges,
        scratch=[pltpu.VMEM((lay.rows, lay.rows), F32)],
        flops=2 * edge_src.shape[0] * lay.rows * lay.rows,
    )
    message = call(
        forward_body,
        [((lay.rows, hid), BF16)],
        [table, w_edge_in, low, high, count_rows],
    )
    back = lax.all_to_all(message, "dev", 0, 0, tiled=True)
    slope, table_t = call(
        body(slope_body, n_group, n_dev),
        [((lay.rows, hid), F32), ((width, lay.rows), BF16)],
        [table, w_edge_in],
        flops=2 * lay.rows * width * hid,
    )

    hub_part = call(body(hub_sum_body, lay), [((hubs, hid + 128), F32)], [back])
    group_cube = Cube(n_group, n_dev, [("group", 1, n_group)])
    parts = [hub_part] + [group_cube.send(hub_part, step) for step in range(1, n_group)]

    def row_outs(count):
        return [
            ((count, width), BF16),
            ((count, width), BF16),
            ((count, width), BF16),
            ((count, hid), BF16),
            ((count, hid), BF16),
            ((count, width), BF16),
        ]

    new_state, *saved, grad_rows = call(
        body(master_body, lay),
        row_outs(rows) + [((lay.rows, hid), F32)],
        [chosen, back, node_state, node_cot, w_edge_out, w_update],
        flops=2 * rows * (2 * lay.rows * hid + 2 * width * width + 2 * width * hid),
    )
    new_hub, *hub_saved, grad_message = call(
        body(hub_body, lay, n_group),
        row_outs(hubs) + [((lay.rows, hid), BF16)],
        parts + [hub_state, hub_cot, w_edge_out, w_update, grad_rows],
    )
    grad_table = lax.all_to_all(grad_message, "dev", 0, 0, tiled=True)

    weight = (lax.axis_index("group") == 0).astype(I32).reshape(1)
    upper = call(
        weight_body,
        [((width + hid, width), F32)],
        [weight] + saved + hub_saved,
        flops=2 * rows * width * (width + 2 * hid),
        smem=1,
    )
    side = call(
        backward_body,
        [((width, hid), BF16)],
        [grad_table, low_t, high_t, slope, table_t],
        flops=2 * lay.rows * hid * (lay.rows + width) * 2,
    )
    core = Cube(n_group, n_dev, [("group", 1, 2)])
    flat = Cube(n_group, n_dev, [("group", 2, n_group // 2), ("dev", 1, 2)])
    line = Cube(n_group, n_dev, [("dev", 2, n_dev // 2)])
    upper = total(*core.scatter(upper))
    upper, terms = flat.scatter(upper)
    terms, side = lax.optimization_barrier((terms, side))
    upper = total(upper, terms)
    upper = total(*line.scatter(upper)).astype(BF16)

    side = lax.all_to_all(side, both, 0, 0, tiled=True)
    own = jnp.sum(side.reshape(n_group * n_dev, -1, hid).astype(F32), axis=0).astype(BF16)
    depth = own.shape[0] // 2
    own = jnp.concatenate([own[:depth], own[depth:]], axis=1)
    whole = jnp.concatenate([upper, own], axis=0)
    for cube in (line, flat, core):
        whole = cube.gather(whole)
    whole = whole.reshape(n_group * n_dev, -1, width).astype(F32)
    split = whole.shape[1] - depth
    upper = whole[:, :split].reshape(-1, width)
    side = whole[:, split:]
    side = jnp.concatenate([side[:, :, :hid], side[:, :, hid:]], axis=1).reshape(width, hid)
    return new_state, new_hub, side, upper[width:], upper[:width]


def solution(mesh):
    def body(*args):
        return shards(*args, n_group=mesh.shape["group"], n_dev=mesh.shape["dev"])

    return jax.shard_map(
        body,
        mesh=mesh,
        in_specs=(
            P(("group", "dev"), None),
            P("dev", None),
            P(),
            P(),
            P(),
            P(("group", "dev")),
            P(("group", "dev")),
            P(("group", "dev")),
            P(("group", "dev"), None, None),
            P(("group", "dev"), None),
            P(("group", "dev"), None),
            P("dev", None),
        ),
        out_specs=(P(("group", "dev"), None), P("dev", None), P(), P(), P()),
        check_vma=False,
    )
```

time: 418 us -> 97 us (0.23)
  waiting for transfers between devices: 178 us -> 36.2 us
  blocking collectives: 89.5 us -> 0 us
  local copies, waits for them, and re-layouts: 59.5 us -> 7.7 us
  matrix products: 51.1 us -> 0 us
  starting transfers between devices: 19.8 us -> 36.3 us
  between operations: 14.9 us -> 0.95 us
  Pallas kernels: 0 us -> 12 us
    psum x1 -> x0, waiting for transfers between devices: 133 us -> none  [shards(): lax.psum((local_grads[0], local_grads[1], grad_update), ('group', 'dev'))]
    all_gather x2 -> x0, blocking collectives: 61.7 us -> none  [the longest x1 31.2 us: shards(): hub_table = lax.all_gather(hub_state, 'dev', axis=0, tiled=True)]
    dot_general x25 -> x0, matrix products: 51.1 us -> none  [the longest x4 13.6 us: backward_step(): lax.dot_general(gathered, grad_act, contract, preferred_element_type=jnp....]
    gather x12 -> x0, local copies, waits for them, and re-layouts: 47.6 us -> none  [the longest x4 15.9 us: backward_step(): grad_table[target_ids]]
    reduce_scatter x1 -> x0, waiting for transfers between devices: 38.2 us -> none  [shards(): lax.psum_scatter(whole_part.astype(jnp.bfloat16), 'dev', scatter_dimensio...]
    unnamed x1 -> x0, blocking collectives: 21.8 us -> none
    ppermute x0 -> x17, starting transfers between devices: none -> 18.3 us  [send(): return lax.ppermute(value, ('group', 'dev'), pairs)]
    ppermute x0 -> x17, waiting for transfers between devices: none -> 15.8 us  [send(): return lax.ppermute(value, ('group', 'dev'), pairs)]
  transfers between devices with their start and end apart: 6 -> 21, of which waited for: 3 -> 12; matrix products, arithmetic and copies ran while one was open for 2% -> 1% of each run, Pallas kernels for 0% -> 7%
where the time goes in v2:
time: 97 us; the launch traced here: 96.3 us
  starting transfers between devices  36.3 us (37%)
  waiting for transfers between devices  36.2 us (37%)
  Pallas kernels  12 us (12%)
  local copies, waits for them, and re-layouts  7.7 us (8%)
  other arithmetic  3.27 us (3%)
    ppermute x17, starting transfers between devices, send(): return lax.ppermute(value, ('group', 'dev'), pairs)  18.3 us
    ppermute x17, waiting for transfers between devices, send(): return lax.ppermute(value, ('group', 'dev'), pairs)  15.8 us
    pallas_call x9, Pallas kernels, call(): pl.pallas_call(body, out_shape=outs[0] if single else outs, in_specs=spec...  12 us
    all_to_all x1, waiting for transfers between devices, shards(): table = lax.all_to_all(packed, 'dev', 0, 0, tiled=True)  9.24 us
    all_to_all x1, waiting for transfers between devices, shards(): back = lax.all_to_all(message, 'dev', 0, 0, tiled=True)  7.81 us
    all_to_all x1, starting transfers between devices, shards(): table = lax.all_to_all(packed, 'dev', 0, 0, tiled=True)  7.25 us
    unnamed x28, local copies, waits for them, and re-layouts  4.64 us
    all_to_all x1, starting transfers between devices, shards(): side = lax.all_to_all(side, both, 0, 0, tiled=True)  3.7 us
  transfers between devices with their start and end apart: 21, of which 12 were waited for; matrix products, arithmetic and copies ran while one was open for 1% of the time, Pallas kernels for 7%

profile of v2, /device:TPU:0, one launch (start us, length us, event | category | flops | bytes accessed | tf_op | source)
XLA Modules:
  0.0 96.3 jit_solution(1237696946133561237)
XLA Ops:
  4.4 7.3 %all-to-all-start = ((bf16[8,48,512]{2,1,0:T(8,128)(2,1)}), bf16[8,48,512]{2,1,0:T(8,128)(2,1)S(1)}, u32[]{:S(2)}, u32[]{:S(2)}) async-start(bf16[8,48,512]{2,1,0:T(8,128)(2,1)} %bitcast.2), calls=%async_computation | async-start | bytes 786432 | tf_op jit(solution)/shard_map/all_to_all | solution.py:365
  11.7 2.3 %shard_map.156 = (bf16[384,384]{1,0:T(8,128)(2,1)S(1)}, bf16[384,384]{1,0:T(8,128)(2,1)S(1)}, bf16[384,384]{1,0:T(8,128)(2,1)S(1)}, bf16[384,384]{1,0:T(8,128)(2,1)S(1)}, bf16[384,256]{1,0:T(8,128)(2,1)S(1)}) custom-call(s32[8,512]{1,0:T(8,128)S(1)} %reshape.64.src_ref, s32[8,512]{1,0:T(8,128)S(1)} %reshape.65.dst_ref, s32[8,512]{1,0:T(8,128)S(1)} %reshape.66.mask_ref), custom_call_target="tpu_custom_call" | custom-call | flops 1207959552 | bytes 1425408 | tf_op jit(solution)/shard_map/pallas_call | solution.py:276
  14.1 9.2 %all-to-all-done = bf16[8,48,512]{2,1,0:T(8,128)(2,1)S(1)} async-done(((bf16[8,48,512]{2,1,0:T(8,128)(2,1)}), bf16[8,48,512]{2,1,0:T(8,128)(2,1)S(1)}, u32[]{:S(2)}, u32[]{:S(2)}) %all-to-all-start) | async-done | bytes 393248 | tf_op jit(solution)/shard_map/all_to_all | solution.py:365
  24.6 3.6 %all-to-all-start.1 = ((bf16[8,48,256]{2,1,0:T(8,128)(2,1)}), bf16[8,48,256]{2,1,0:T(8,128)(2,1)S(1)}, u32[]{:S(2)}, u32[]{:S(2)}) async-start(bf16[8,48,256]{2,1,0:T(8,128)(2,1)} %bitcast.4), calls=%async_computation.1 | async-start | bytes 393216 | tf_op jit(solution)/shard_map/all_to_all | solution.py:382
  28.2 7.8 %all-to-all-done.1 = bf16[8,48,256]{2,1,0:T(8,128)(2,1)S(1)} async-done(((bf16[8,48,256]{2,1,0:T(8,128)(2,1)}), bf16[8,48,256]{2,1,0:T(8,128)(2,1)S(1)}, u32[]{:S(2)}, u32[]{:S(2)}) %all-to-all-start.1) | async-done | bytes 196640 | tf_op jit(solution)/shard_map/all_to_all | solution.py:382
  36.1 1.6 %collective-permute-start.1 = (f32[8,384]{1,0:T(8,128)S(1)}, f32[8,384]{1,0:T(8,128)S(1)}, u32[]{:S(2)}, u32[]{:S(2)}) collective-permute-start(f32[8,384]{1,0:T(8,128)S(1)} %shard_map.159.refs_0_), channel_id=1, source_target_pairs={{0,16},{1,17},{2,18},{3,19},{4,20},{5,21},{6,22},{7,23},{8,24},{9,... | collective-permute-start | bytes 36872 | tf_op jit(solution)/shard_map/ppermute | solution.py:305
  40.0 2.6 %shard_map.158 = (bf16[512,512]{1,0:T(8,128)(2,1)}, bf16[512,512]{1,0:T(8,128)(2,1)S(1)}, bf16[512,512]{1,0:T(8,128)(2,1)S(1)}, bf16[512,256]{1,0:T(8,128)(2,1)S...) custom-call(s32[1,384]{1,0:T(1,128)S(1)} %reshape.63.chosen_ref, ...), custom_call_target="tpu_custom_call" | custom-call | flops 1006632960 | bytes 5047808 | tf_op jit(solution)/shard_map/pallas_call | solution.py:276
  42.7 1.4 %shard_map.160 = (bf16[8,512]{1,0:T(8,128)(2,1)}, bf16[8,512]{1,0:T(8,128)(2,1)S(1)}, bf16[8,512]{1,0:T(8,128)(2,1)S(1)}, bf16[8,256]{1,0:T(8,128)(2,1)S(1)}, bf...) custom-call(f32[8,384]{1,0:T(8,128)S(1)} %shard_map.159.refs_0_, ...), custom_call_target="tpu_custom_call" | custom-call | bytes 1482752 | tf_op jit(solution)/shard_map/pallas_call | solution.py:276
  46.2 3.4 %all-to-all-start.2 = ((bf16[8,48,256]{2,1,0:T(8,128)(2,1)}), bf16[8,48,256]{2,1,0:T(8,128)(2,1)S(1)}, u32[]{:S(2)}, u32[]{:S(2)}) async-start(bf16[8,48,256]{2,1,0:T(8,128)(2,1)} %bitcast.15), calls=%async_computation.2 | async-start | bytes 393216 | tf_op jit(solution)/shard_map/all_to_all | solution.py:415
  50.7 2.0 %collective-permute-start.4 = (bf16[96,512]{1,0:T(8,128)(2,1)S(1)}, bf16[96,512]{1,0:T(8,128)(2,1)S(1)}, u32[]{:S(2)}, u32[]{:S(2)}) collective-permute-start(bf16[96,512]{1,0:T(8,128)(2,1)S(1)} %get-tuple-element.61), channel_id=1, source_target_pairs={{0,1},{1,0},{2,3},{3,2},{4,5},{5,4},{6,7},{7,6},{8,9},{9,8},{10,11... | collective-permute-start | bytes 294920 | tf_op jit(solution)/shard_map/ppermute | solution.py:305
  52.7 1.5 %collective-permute-start.5 = (bf16[96,512]{1,0:T(8,128)(2,1)S(1)}, bf16[96,512]{1,0:T(8,128)(2,1)S(1)}, u32[]{:S(2)}, u32[]{:S(2)}) collective-permute-start(bf16[96,512]{1,0:T(8,128)(2,1)S(1)} %get-tuple-element.60), channel_id=1, source_target_pairs={{0,16},{1,17},{2,18},{3,19},{4,20},{5,21},{6,22},{7,23},{8,24},{9,... | collective-permute-start | bytes 294920 | tf_op jit(solution)/shard_map/ppermute | solution.py:305
  54.9 3.4 %all-to-all-done.2 = bf16[8,48,256]{2,1,0:T(8,128)(2,1)S(1)} async-done(((bf16[8,48,256]{2,1,0:T(8,128)(2,1)}), bf16[8,48,256]{2,1,0:T(8,128)(2,1)S(1)}, u32[]{:S(2)}, u32[]{:S(2)}) %all-to-all-start.2) | async-done | bytes 196640 | tf_op jit(solution)/shard_map/all_to_all | solution.py:415
  58.2 1.4 %shard_map.163 = bf16[512,256]{1,0:T(8,128)(2,1)} custom-call(bf16[384,256]{1,0:T(8,128)(2,1)S(1)} %bitcast.52, bf16[384,384]{1,0:T(8,128)(2,1)S(1)} %get-tuple-element.47.low_ref, bf16[384,384]{1,0:T(8,128)(2,1)S(1)} %get-tuple-element.48.high_ref, f32[384,256]{1,0:T(8,128)S(1)} %get-tuple-element.49.slope_ref, ...), custom_call_target="tpu_custom_call" | custom-call | flops 352321536 | bytes 1835008 | tf_op jit(solution)/shard_map/pallas_call | solution.py:276
  60.3 3.7 %all-to-all-start.3 = ((bf16[32,16,256]{2,1,0:T(8,128)(2,1)}), bf16[32,16,256]{2,1,0:T(8,128)(2,1)S(1)}, u32[]{:S(2)}, u32[]{:S(2)}) async-start(bf16[32,16,256]{2,1,0:T(8,128)(2,1)} %bitcast.22), calls=%async_computation.3 | async-start | bytes 524288 | tf_op jit(solution)/shard_map/all_to_all | solution.py:440
  65.0 1.8 %collective-permute-start.7 = (bf16[24,512]{1,0:T(8,128)(2,1)S(1)}, bf16[24,512]{1,0:T(8,128)(2,1)S(1)}, u32[]{:S(2)}, u32[]{:S(2)}) collective-permute-start(bf16[24,512]{1,0:T(8,128)(2,1)S(1)} %get-tuple-element.65), channel_id=1, source_target_pairs={{0,2},{1,3},{2,0},{3,1},{4,6},{5,7},{6,4},{7,5},{8,10},{9,11},{10,... | collective-permute-start | bytes 73736 | tf_op jit(solution)/shard_map/ppermute | solution.py:305
  66.9 2.4 %collective-permute-start.8 = (bf16[24,512]{1,0:T(8,128)(2,1)S(1)}, bf16[24,512]{1,0:T(8,128)(2,1)S(1)}, u32[]{:S(2)}, u32[]{:S(2)}) collective-permute-start(bf16[24,512]{1,0:T(8,128)(2,1)S(1)} %get-tuple-element.67), channel_id=1, source_target_pairs={{0,4},{1,5},{2,6},{3,7},{4,0},{5,1},{6,2},{7,3},{8,12},{9,13},{10,... | collective-permute-start | bytes 73736 | tf_op jit(solution)/shard_map/ppermute | solution.py:305
  69.7 5.6 %collective-permute-done.8 = bf16[24,512]{1,0:T(8,128)(2,1)S(1)} collective-permute-done((bf16[24,512]{1,0:T(8,128)(2,1)S(1)}, bf16[24,512]{1,0:T(8,128)(2,1)S(1)}, u32[]{:S(2)}, u32[]{:S(2)}) %collective-permute-start.8) | collective-permute-done | bytes 24608 | tf_op jit(solution)/shard_map/ppermute | solution.py:305
  75.4 1.7 %collective-permute-start.10 = (bf16[32,512]{1,0:T(8,128)(2,1)S(1)}, bf16[32,512]{1,0:T(8,128)(2,1)S(1)}, u32[]{:S(2)}, u32[]{:S(2)}) collective-permute-start(bf16[32,512]{1,0:T(8,128)(2,1)S(1)} %maximum_maximum_fusion), channel_id=1, source_target_pairs={{0,6},{1,7},{2,4},{3,5},{4,2},{5,3},{6,0},{7,1},{8,14},{9,15},{10,... | collective-permute-start | bytes 98312 | tf_op jit(solution)/shard_map/ppermute | solution.py:305
  77.0 1.3 %collective-permute-start.11 = (bf16[32,512]{1,0:T(8,128)(2,1)S(1)}, bf16[32,512]{1,0:T(8,128)(2,1)S(1)}, u32[]{:S(2)}, u32[]{:S(2)}) collective-permute-start(bf16[32,512]{1,0:T(8,128)(2,1)S(1)} %maximum_maximum_fusion), channel_id=1, source_target_pairs={{0,4},{1,5},{2,6},{3,7},{4,0},{5,1},{6,2},{7,3},{8,12},{9,13},{10,... | collective-permute-start | bytes 98312 | tf_op jit(solution)/shard_map/ppermute | solution.py:305
  78.3 1.5 %collective-permute-start.12 = (bf16[32,512]{1,0:T(8,128)(2,1)S(1)}, bf16[32,512]{1,0:T(8,128)(2,1)S(1)}, u32[]{:S(2)}, u32[]{:S(2)}) collective-permute-start(bf16[32,512]{1,0:T(8,128)(2,1)S(1)} %maximum_maximum_fusion), channel_id=1, source_target_pairs={{0,2},{1,3},{2,0},{3,1},{4,6},{5,7},{6,4},{7,5},{8,10},{9,11},{10,... | collective-permute-start | bytes 98312 | tf_op jit(solution)/shard_map/ppermute | solution.py:305
  79.8 1.6 %collective-permute-done.10 = bf16[32,512]{1,0:T(8,128)(2,1)S(1)} collective-permute-done((bf16[32,512]{1,0:T(8,128)(2,1)S(1)}, bf16[32,512]{1,0:T(8,128)(2,1)S(1)}, u32[]{:S(2)}, u32[]{:S(2)}) %collective-permute-start.10) | collective-permute-done | bytes 32800 | tf_op jit(solution)/shard_map/ppermute | solution.py:305
  82.6 1.8 %collective-permute-start.13 = (bf16[128,512]{1,0:T(8,128)(2,1)S(1)}, bf16[128,512]{1,0:T(8,128)(2,1)S(1)}, u32[]{:S(2)}, u32[]{:S(2)}) collective-permute-start(bf16[128,512]{1,0:T(8,128)(2,1)S(1)} %pad_maximum_fusion.3), channel_id=1, source_target_pairs={{0,17},{1,16},{2,19},{3,18},{4,21},{5,20},{6,23},{7,22},{8,25},{9,... | collective-permute-start | bytes 393224 | tf_op jit(solution)/shard_map/ppermute | solution.py:305
  86.2 3.8 %collective-permute-done.13 = bf16[128,512]{1,0:T(8,128)(2,1)S(1)} collective-permute-done((bf16[128,512]{1,0:T(8,128)(2,1)S(1)}, bf16[128,512]{1,0:T(8,128)(2,1)S(1)}, u32[]{:S(2)}, u32[]{:S(2)}) %collective-permute-start.13) | collective-permute-done | bytes 131104 | tf_op jit(solution)/shard_map/ppermute | solution.py:305
  91.2 1.9 %collective-permute-done.16 = bf16[512,512]{1,0:T(8,128)(2,1)S(1)} collective-permute-done((bf16[512,512]{1,0:T(8,128)(2,1)S(1)}, bf16[512,512]{1,0:T(8,128)(2,1)S(1)}, u32[]{:S(2)}, u32[]{:S(2)}) %collective-permute-start.16) | collective-permute-done | bytes 524320 | tf_op jit(solution)/shard_map/ppermute | solution.py:305
  (82 shorter events, 20.7 us)
Async XLA Ops:
  4.4 18.9 %all-to-all-start = ((bf16[8,48,512]{2,1,0:T(8,128)(2,1)}), bf16[8,48,512]{2,1,0:T(8,128)(2,1)S(1)}, u32[]{:S(2)}, u32[]{:S(2)}) async-start(bf16[8,48,512]{2,1,0:T(8,128)(2,1)} %bitcast.2), calls=%async_computation | async-start | bytes 786432 | tf_op jit(solution)/shard_map/all_to_all | solution.py:365
  11.7 11.6 %copy-start = (bf16[512,256]{1,0:T(8,128)(2,1)S(1)}, bf16[512,256]{1,0:T(8,128)(2,1)}, u32[]{:S(2)}) copy-start(bf16[512,256]{1,0:T(8,128)(2,1)} %w_ref.3) | copy-start | bytes 786436
  14.1 23.9 %copy-start.2 = (bf16[512,512]{1,0:T(8,128)(2,1)S(1)}, bf16[512,512]{1,0:T(8,128)(2,1)}, u32[]{:S(2)}) copy-start(bf16[512,512]{1,0:T(8,128)(2,1)} %state_ref.1) | copy-start | bytes 1572868
  14.1 23.9 %copy-start.3 = (bf16[512,512]{1,0:T(8,128)(2,1)S(1)}, bf16[512,512]{1,0:T(8,128)(2,1)}, u32[]{:S(2)}) copy-start(bf16[512,512]{1,0:T(8,128)(2,1)} %refs_7_.1) | copy-start | bytes 1572868
  24.6 11.4 %all-to-all-start.1 = ((bf16[8,48,256]{2,1,0:T(8,128)(2,1)}), bf16[8,48,256]{2,1,0:T(8,128)(2,1)S(1)}, u32[]{:S(2)}, u32[]{:S(2)}) async-start(bf16[8,48,256]{2,1,0:T(8,128)(2,1)} %bitcast.4), calls=%async_computation.1 | async-start | bytes 393216 | tf_op jit(solution)/shard_map/all_to_all | solution.py:382
  36.1 6.5 %collective-permute-start = (f32[8,384]{1,0:T(8,128)S(1)}, f32[8,384]{1,0:T(8,128)S(1)}, u32[]{:S(2)}, u32[]{:S(2)}) collective-permute-start(f32[8,384]{1,0:T(8,128)S(1)} %shard_map.159.refs_0_), channel_id=1, source_target_pairs={{0,8},{1,9},{2,10},{3,11},{4,12},{5,13},{6,14},{7,15},{8,0},{9,1},... | collective-permute-start | bytes 36872 | tf_op jit(solution)/shard_map/ppermute | solution.py:305
  36.1 6.5 %collective-permute-start.1 = (f32[8,384]{1,0:T(8,128)S(1)}, f32[8,384]{1,0:T(8,128)S(1)}, u32[]{:S(2)}, u32[]{:S(2)}) collective-permute-start(f32[8,384]{1,0:T(8,128)S(1)} %shard_map.159.refs_0_), channel_id=1, source_target_pairs={{0,16},{1,17},{2,18},{3,19},{4,20},{5,21},{6,22},{7,23},{8,24},{9,... | collective-permute-start | bytes 36872 | tf_op jit(solution)/shard_map/ppermute | solution.py:305
  37.7 4.9 %collective-permute-start.2 = (f32[8,384]{1,0:T(8,128)S(1)}, f32[8,384]{1,0:T(8,128)S(1)}, u32[]{:S(2)}, u32[]{:S(2)}) collective-permute-start(f32[8,384]{1,0:T(8,128)S(1)} %shard_map.159.refs_0_), channel_id=1, source_target_pairs={{0,24},{1,25},{2,26},{3,27},{4,28},{5,29},{6,30},{7,31},{8,16},{9,... | collective-permute-start | bytes 36872 | tf_op jit(solution)/shard_map/ppermute | solution.py:305
  45.9 3.8 %collective-permute-start.3 = (bf16[384,512]{1,0:T(8,128)(2,1)}, bf16[384,512]{1,0:T(8,128)(2,1)S(1)}, u32[]{:S(2)}, u32[]{:S(2)}) collective-permute-start(bf16[384,512]{1,0:T(8,128)(2,1)} %fusion), channel_id=1, source_target_pairs={{0,8},{1,9},{2,10},{3,11},{4,12},{5,13},{6,14},{7,15},{8,0},{9,1},... | collective-permute-start | bytes 1179656 | tf_op jit(solution)/shard_map/ppermute | solution.py:305
  46.2 12.0 %all-to-all-start.2 = ((bf16[8,48,256]{2,1,0:T(8,128)(2,1)}), bf16[8,48,256]{2,1,0:T(8,128)(2,1)S(1)}, u32[]{:S(2)}, u32[]{:S(2)}) async-start(bf16[8,48,256]{2,1,0:T(8,128)(2,1)} %bitcast.15), calls=%async_computation.2 | async-start | bytes 393216 | tf_op jit(solution)/shard_map/all_to_all | solution.py:415
  50.7 9.0 %collective-permute-start.4 = (bf16[96,512]{1,0:T(8,128)(2,1)S(1)}, bf16[96,512]{1,0:T(8,128)(2,1)S(1)}, u32[]{:S(2)}, u32[]{:S(2)}) collective-permute-start(bf16[96,512]{1,0:T(8,128)(2,1)S(1)} %get-tuple-element.61), channel_id=1, source_target_pairs={{0,1},{1,0},{2,3},{3,2},{4,5},{5,4},{6,7},{7,6},{8,9},{9,8},{10,11... | collective-permute-start | bytes 294920 | tf_op jit(solution)/shard_map/ppermute | solution.py:305
  52.7 7.0 %collective-permute-start.5 = (bf16[96,512]{1,0:T(8,128)(2,1)S(1)}, bf16[96,512]{1,0:T(8,128)(2,1)S(1)}, u32[]{:S(2)}, u32[]{:S(2)}) collective-permute-start(bf16[96,512]{1,0:T(8,128)(2,1)S(1)} %get-tuple-element.60), channel_id=1, source_target_pairs={{0,16},{1,17},{2,18},{3,19},{4,20},{5,21},{6,22},{7,23},{8,24},{9,... | collective-permute-start | bytes 294920 | tf_op jit(solution)/shard_map/ppermute | solution.py:305
  54.2 6.1 %collective-permute-start.6 = (bf16[96,512]{1,0:T(8,128)(2,1)S(1)}, bf16[96,512]{1,0:T(8,128)(2,1)S(1)}, u32[]{:S(2)}, u32[]{:S(2)}) collective-permute-start(bf16[96,512]{1,0:T(8,128)(2,1)S(1)} %get-tuple-element.59), channel_id=1, source_target_pairs={{0,17},{1,16},{2,19},{3,18},{4,21},{5,20},{6,23},{7,22},{8,25},{9,... | collective-permute-start | bytes 294920 | tf_op jit(solution)/shard_map/ppermute | solution.py:305
  60.3 15.0 %all-to-all-start.3 = ((bf16[32,16,256]{2,1,0:T(8,128)(2,1)}), bf16[32,16,256]{2,1,0:T(8,128)(2,1)S(1)}, u32[]{:S(2)}, u32[]{:S(2)}) async-start(bf16[32,16,256]{2,1,0:T(8,128)(2,1)} %bitcast.22), calls=%async_computation.3 | async-start | bytes 524288 | tf_op jit(solution)/shard_map/all_to_all | solution.py:440
  65.0 4.6 %collective-permute-start.7 = (bf16[24,512]{1,0:T(8,128)(2,1)S(1)}, bf16[24,512]{1,0:T(8,128)(2,1)S(1)}, u32[]{:S(2)}, u32[]{:S(2)}) collective-permute-start(bf16[24,512]{1,0:T(8,128)(2,1)S(1)} %get-tuple-element.65), channel_id=1, source_target_pairs={{0,2},{1,3},{2,0},{3,1},{4,6},{5,7},{6,4},{7,5},{8,10},{9,11},{10,... | collective-permute-start | bytes 73736 | tf_op jit(solution)/shard_map/ppermute | solution.py:305
  66.9 8.4 %collective-permute-start.8 = (bf16[24,512]{1,0:T(8,128)(2,1)S(1)}, bf16[24,512]{1,0:T(8,128)(2,1)S(1)}, u32[]{:S(2)}, u32[]{:S(2)}) collective-permute-start(bf16[24,512]{1,0:T(8,128)(2,1)S(1)} %get-tuple-element.67), channel_id=1, source_target_pairs={{0,4},{1,5},{2,6},{3,7},{4,0},{5,1},{6,2},{7,3},{8,12},{9,13},{10,... | collective-permute-start | bytes 73736 | tf_op jit(solution)/shard_map/ppermute | solution.py:305
  69.3 6.0 %collective-permute-start.9 = (bf16[24,512]{1,0:T(8,128)(2,1)S(1)}, bf16[24,512]{1,0:T(8,128)(2,1)S(1)}, u32[]{:S(2)}, u32[]{:S(2)}) collective-permute-start(bf16[24,512]{1,0:T(8,128)(2,1)S(1)} %get-tuple-element.66), channel_id=1, source_target_pairs={{0,6},{1,7},{2,4},{3,5},{4,2},{5,3},{6,0},{7,1},{8,14},{9,15},{10,... | collective-permute-start | bytes 73736 | tf_op jit(solution)/shard_map/ppermute | solution.py:305
  75.4 6.0 %collective-permute-start.10 = (bf16[32,512]{1,0:T(8,128)(2,1)S(1)}, bf16[32,512]{1,0:T(8,128)(2,1)S(1)}, u32[]{:S(2)}, u32[]{:S(2)}) collective-permute-start(bf16[32,512]{1,0:T(8,128)(2,1)S(1)} %maximum_maximum_fusion), channel_id=1, source_target_pairs={{0,6},{1,7},{2,4},{3,5},{4,2},{5,3},{6,0},{7,1},{8,14},{9,15},{10,... | collective-permute-start | bytes 98312 | tf_op jit(solution)/shard_map/ppermute | solution.py:305
  77.0 5.3 %collective-permute-start.11 = (bf16[32,512]{1,0:T(8,128)(2,1)S(1)}, bf16[32,512]{1,0:T(8,128)(2,1)S(1)}, u32[]{:S(2)}, u32[]{:S(2)}) collective-permute-start(bf16[32,512]{1,0:T(8,128)(2,1)S(1)} %maximum_maximum_fusion), channel_id=1, source_target_pairs={{0,4},{1,5},{2,6},{3,7},{4,0},{5,1},{6,2},{7,3},{8,12},{9,13},{10,... | collective-permute-start | bytes 98312 | tf_op jit(solution)/shard_map/ppermute | solution.py:305
  78.3 4.3 %collective-permute-start.12 = (bf16[32,512]{1,0:T(8,128)(2,1)S(1)}, bf16[32,512]{1,0:T(8,128)(2,1)S(1)}, u32[]{:S(2)}, u32[]{:S(2)}) collective-permute-start(bf16[32,512]{1,0:T(8,128)(2,1)S(1)} %maximum_maximum_fusion), channel_id=1, source_target_pairs={{0,2},{1,3},{2,0},{3,1},{4,6},{5,7},{6,4},{7,5},{8,10},{9,11},{10,... | collective-permute-start | bytes 98312 | tf_op jit(solution)/shard_map/ppermute | solution.py:305
  82.6 7.3 %collective-permute-start.13 = (bf16[128,512]{1,0:T(8,128)(2,1)S(1)}, bf16[128,512]{1,0:T(8,128)(2,1)S(1)}, u32[]{:S(2)}, u32[]{:S(2)}) collective-permute-start(bf16[128,512]{1,0:T(8,128)(2,1)S(1)} %pad_maximum_fusion.3), channel_id=1, source_target_pairs={{0,17},{1,16},{2,19},{3,18},{4,21},{5,20},{6,23},{7,22},{8,25},{9,... | collective-permute-start | bytes 393224 | tf_op jit(solution)/shard_map/ppermute | solution.py:305
  84.5 6.5 %collective-permute-start.14 = (bf16[128,512]{1,0:T(8,128)(2,1)S(1)}, bf16[128,512]{1,0:T(8,128)(2,1)S(1)}, u32[]{:S(2)}, u32[]{:S(2)}) collective-permute-start(bf16[128,512]{1,0:T(8,128)(2,1)S(1)} %pad_maximum_fusion.3), channel_id=1, source_target_pairs={{0,16},{1,17},{2,18},{3,19},{4,20},{5,21},{6,22},{7,23},{8,24},{9,... | collective-permute-start | bytes 393224 | tf_op jit(solution)/shard_map/ppermute | solution.py:305
  85.2 5.7 %collective-permute-start.15 = (bf16[128,512]{1,0:T(8,128)(2,1)S(1)}, bf16[128,512]{1,0:T(8,128)(2,1)S(1)}, u32[]{:S(2)}, u32[]{:S(2)}) collective-permute-start(bf16[128,512]{1,0:T(8,128)(2,1)S(1)} %pad_maximum_fusion.3), channel_id=1, source_target_pairs={{0,1},{1,0},{2,3},{3,2},{4,5},{5,4},{6,7},{7,6},{8,9},{9,8},{10,11... | collective-permute-start | bytes 393224 | tf_op jit(solution)/shard_map/ppermute | solution.py:305
  91.2 2.0 %collective-permute-start.16 = (bf16[512,512]{1,0:T(8,128)(2,1)S(1)}, bf16[512,512]{1,0:T(8,128)(2,1)S(1)}, u32[]{:S(2)}, u32[]{:S(2)}) collective-permute-start(bf16[512,512]{1,0:T(8,128)(2,1)S(1)} %pad_maximum_fusion.1), channel_id=1, source_target_pairs={{0,8},{1,9},{2,10},{3,11},{4,12},{5,13},{6,14},{7,15},{8,0},{9,1},... | collective-permute-start | bytes 1572872 | tf_op jit(solution)/shard_map/ppermute | solution.py:305
  (11 other events, 48.4 us)

commit v3 on v2

v3 whole, which is shorter than its diff:
```python
import functools

import jax
import jax.numpy as jnp
from jax import lax
from jax.experimental import pallas as pl
from jax.experimental.pallas import tpu as pltpu
from jax.sharding import PartitionSpec as P

F32 = jnp.float32
BF16 = jnp.bfloat16
I32 = jnp.int32
CHUNK = 512
NN = ((1,), (0,))
NT = ((1,), (1,))
TN = ((0,), (0,))


def dot(left, right, dims=NN):
    return lax.dot_general(left, right, (dims, ((), ())), preferred_element_type=F32)


def halves(value):
    high = value.astype(BF16)
    return high, (value - high.astype(F32)).astype(BF16)


def silu(values):
    return values * jax.nn.sigmoid(values)


def silu_grad(values):
    sigmoid_v = jax.nn.sigmoid(values)
    return sigmoid_v * (1.0 + values * (1.0 - sigmoid_v))


def iota(shape, axis):
    return lax.broadcasted_iota(I32, shape, axis)


class Layout:
    def __init__(self, peers, slots, hubs):
        self.peers, self.slots, self.hubs = peers, slots, hubs
        self.block = slots + hubs
        self.wide = -(-(self.block + 2) // 16) * 16
        self.rows, self.wide_rows = peers * self.block, peers * self.wide

    def place(self, ids):
        mirrors = self.peers * self.slots
        slot_bits, hub_bits = self.slots.bit_length() - 1, self.hubs.bit_length() - 1
        hub_ids = ids - mirrors
        mirror_row = (ids >> slot_bits) * self.block + (ids & (self.slots - 1))
        hub_row = (hub_ids >> hub_bits) * self.block + self.slots + (hub_ids & (self.hubs - 1))
        return jnp.where(ids < mirrors, mirror_row, hub_row)

    def join(self, rows, hubs):
        parts = []
        for peer in range(self.peers):
            start = peer * self.block
            parts += [rows[start : start + self.slots], hubs]
        return jnp.concatenate(parts, axis=0)


def block_of(shape, axis, block):
    index = iota(shape, axis).astype(F32)
    number = jnp.floor((index + 0.5) * (1.0 / block))
    return number, index - block * number


def choose(lay, block, count_ref, list_ref):
    _, col_rest = block_of((lay.slots, lay.peers * block), 1, block)
    spread = (col_rest == iota(col_rest.shape, 0).astype(F32)).astype(BF16)
    wanted = list_ref[...]
    high, low = (wanted >> 4).astype(BF16), (wanted & 15).astype(BF16)
    placed = 16.0 * dot(high, spread) + dot(low, spread)
    shape = (lay.peers, lay.peers * block)
    peer, col = iota(shape, 0), iota(shape, 1)
    count = jnp.zeros(shape, I32)
    for index in range(lay.peers):
        count = jnp.where(peer == index, count_ref[0, index], count)
    slot = col - peer * block
    live = (slot >= 0) & (slot < count)
    chosen = jnp.sum(jnp.where(live, placed + 1.0, 0.0), axis=0, keepdims=True) - 1.0
    return chosen.astype(I32)


def gather_body(lay, count_ref, list_ref, rows_ref, hubs_ref, out_ref):
    rows = rows_ref.shape[0]
    chosen = choose(lay, lay.block, count_ref, list_ref)
    select = (iota((rows, lay.rows), 0) == chosen).astype(BF16)
    picked = dot(select, rows_ref[...], TN)
    out_ref[...] = lay.join(picked, hubs_ref[...].astype(F32)).astype(BF16)


def count_body(lay, count_ref, list_ref, src_ref, dst_ref, mask_ref, *refs):
    low_ref, high_ref, rows_ref, near_ref, wide_ref, sum_ref = refs
    chunk = min(CHUNK, src_ref.shape[0])
    steps = src_ref.shape[0] // chunk
    ids = iota((lay.rows, chunk), 0)
    for step in range(steps):
        span = pl.ds(step * chunk, chunk)
        src = lay.place(src_ref[span].reshape(1, chunk))
        keep = mask_ref[span].reshape(1, chunk) > 0
        dst = jnp.where(keep, lay.place(dst_ref[span].reshape(1, chunk)), -1)
        part = dot((ids == dst).astype(BF16), (ids == src).astype(BF16), NT)
        if step == 0:
            sum_ref[...] = part
        else:
            sum_ref[...] += part
    high = jnp.floor(sum_ref[...] * (1.0 / 256.0))
    low = (sum_ref[...] - 256.0 * high).astype(BF16)
    high = high.astype(BF16)
    low_ref[...] = low
    high_ref[...] = high
    ones = jnp.ones((16, lay.rows), BF16)
    counts = (dot(ones, low, NT) + 256.0 * dot(ones, high, NT))[:1]
    rounded = counts.astype(BF16).astype(F32)
    shape = (lay.wide_rows, lay.rows)
    row_block, row_rest = block_of(shape, 0, lay.wide)
    col_block, _ = block_of(shape, 1, lay.block)
    same = row_block == col_block
    spread = jnp.where(same & (row_rest == lay.block), rounded, 0.0)
    spread += jnp.where(same & (row_rest == lay.block + 1), counts - rounded, 0.0)
    _, row_rest = block_of((lay.rows, rows_ref.shape[1]), 0, lay.block)
    fold = (row_rest == iota(row_rest.shape, 1).astype(F32)).astype(BF16)
    rows_ref[...] = dot(spread.astype(BF16), fold).astype(BF16)
    near_ref[...] = choose(lay, lay.block, count_ref, list_ref)
    wide_ref[...] = choose(lay, lay.wide, count_ref, list_ref)


def forward_body(lay, table_ref, w_ref, low_ref, high_ref, rows_ref, out_ref):
    hidden = silu(dot(table_ref[...], w_ref[...])).astype(BF16)
    partial = dot(low_ref[...], hidden) + 256.0 * dot(high_ref[...], hidden)
    rest = jnp.zeros((lay.wide - lay.block, partial.shape[1]), F32)
    parts = []
    for start in range(0, lay.rows, lay.block):
        parts += [partial[start : start + lay.block], rest]
    out_ref[...] = (jnp.concatenate(parts, axis=0) + rows_ref[...].astype(F32)).astype(BF16)


def slope_body(table_ref, w_ref, low_ref, high_ref, slope_ref, table_t_ref, counts_ref):
    slope_ref[...] = silu_grad(dot(table_ref[...], w_ref[...]))

    def turned(ref):
        size = ref.shape[1]
        same = (iota((size, size), 0) == iota((size, size), 1)).astype(BF16)
        return dot(same, ref[...], NT)

    table_t_ref[...] = turned(table_ref).astype(BF16)
    counts_ref[...] = jnp.concatenate([turned(low_ref), turned(high_ref)], axis=0).astype(BF16)


def hub_sum_body(lay, back_ref, out_ref):
    width = back_ref.shape[1]
    hidden = jnp.zeros((lay.hubs, width), F32)
    counts = jnp.zeros((lay.wide - lay.block, width), F32)
    for peer in range(lay.peers):
        start = peer * lay.wide
        part = back_ref[start + lay.slots : start + lay.wide, :].astype(F32)
        hidden += part[: lay.hubs]
        counts += part[lay.hubs :]
    count = counts[0:1] + counts[1:2]
    shape = (lay.hubs, width)
    own = iota(shape, 1) == iota(shape, 0) + lay.slots
    degree = jnp.sum(jnp.where(own, count, 0.0), axis=1, keepdims=True)
    out_ref[:, :width] = hidden
    out_ref[:, width:] = jnp.broadcast_to(degree, (lay.hubs, out_ref.shape[1] - width))


def update_rows(states, cotangent, hidden_sum, degree, w_out, w_update):
    high, low = halves(hidden_sum)
    share = 1.0 / jnp.maximum(degree, 1.0)
    mixed = (states + (dot(high, w_out) + dot(low, w_out)) * share).astype(BF16)
    pre = dot(mixed, w_update)
    updated = (states + silu(pre)).astype(BF16)
    grad_pre = (cotangent * silu_grad(pre)).astype(BF16)
    grad_sum = (dot(grad_pre, w_update, NT) * share).astype(BF16)
    grad_hidden = dot(grad_sum, w_out, NT).astype(BF16)
    return updated, mixed, grad_pre, high, low, grad_sum, grad_hidden


def master_body(lay, n_far, near_ref, wide_ref, back_ref, *refs):
    far, refs = refs[:n_far], refs[n_far:]
    new_ref, mixed_ref, pre_ref, high_ref, low_ref, sum_ref, out_ref = refs[:7]
    near, sems = list(refs[-3:-1]) + list(refs[7:-3]), refs[-1]
    copies = [pltpu.make_async_copy(a, b, sems.at[i]) for i, (a, b) in enumerate(zip(far, near))]
    for copy in copies:
        copy.start()
    state_ref, cot_ref, w_out_ref, w_up_ref = near[:4]
    rows, width = state_ref.shape[0], back_ref.shape[1]
    select = (iota((rows, lay.wide_rows), 0) == wide_ref[...]).astype(BF16)
    back = back_ref[...]
    shape = (lay.wide_rows, lay.wide_rows)
    row_block, _ = block_of(shape, 0, lay.wide)
    taken = iota(shape, 1).astype(F32) == row_block * lay.wide + lay.block
    _, row_rest = block_of((lay.wide_rows, width), 0, lay.wide)
    own = row_rest == iota(row_rest.shape, 1).astype(F32)
    counts = jnp.where(own, dot(taken.astype(BF16), back), 0.0)
    degree = jnp.sum(dot(select, counts.astype(BF16)), axis=1, keepdims=True)
    hidden_sum = dot(select, back)
    for copy in copies:
        copy.wait()
    results = update_rows(
        state_ref[...].astype(F32),
        cot_ref[...].astype(F32),
        hidden_sum,
        degree,
        w_out_ref[...],
        w_up_ref[...],
    )
    updated, mixed, grad_pre, high, low, grad_sum, grad_hidden = results
    select = (iota((rows, lay.rows), 0) == near_ref[...]).astype(BF16)
    out_ref[...] = dot(select, grad_hidden, TN)
    new_ref[...] = updated
    mixed_ref[...] = mixed
    pre_ref[...] = grad_pre
    high_ref[...] = high
    low_ref[...] = low
    sum_ref[...] = grad_sum


def hub_body(
    lay,
    n_parts,
    *refs,
):
    parts = refs[:n_parts]
    state_ref, cot_ref, w_out_ref, w_up_ref, rows_ref = refs[n_parts : n_parts + 5]
    new_ref, mixed_ref, pre_ref, high_ref, low_ref, sum_ref, out_ref = refs[n_parts + 5 :]
    total = parts[0][...]
    for part in parts[1:]:
        total += part[...]
    width = rows_ref.shape[1]
    results = update_rows(
        state_ref[...].astype(F32),
        cot_ref[...].astype(F32),
        total[:, :width],
        total[:, width : width + 1],
        w_out_ref[...],
        w_up_ref[...],
    )
    updated, mixed, grad_pre, high, low, grad_sum, grad_hidden = results
    new_ref[...] = updated
    mixed_ref[...] = mixed
    pre_ref[...] = grad_pre
    high_ref[...] = high
    low_ref[...] = low
    sum_ref[...] = grad_sum
    out_ref[...] = lay.join(rows_ref[...], grad_hidden.astype(F32)).astype(BF16)


def weight_body(
    place_ref,
    mixed_ref,
    pre_ref,
    high_ref,
    low_ref,
    sum_ref,
    hub_mixed_ref,
    hub_pre_ref,
    hub_high_ref,
    hub_low_ref,
    hub_sum_ref,
    *outs,
):
    work = outs[-1]
    weight = place_ref[0].astype(F32)
    rows = mixed_ref.shape[1]
    grad_sum, hub_grad = sum_ref[...], hub_sum_ref[...]
    work[:rows, :] = dot(mixed_ref[...], pre_ref[...], TN) + weight * dot(
        hub_mixed_ref[...], hub_pre_ref[...], TN
    )
    hub_part = dot(hub_high_ref[...], hub_grad, TN) + dot(hub_low_ref[...], hub_grad, TN)
    main = dot(high_ref[...], grad_sum, TN) + dot(low_ref[...], grad_sum, TN)
    work[rows:, :] = main + weight * hub_part
    deal(work, place_ref[1], outs[:-1], len(outs) - 2)


def deal(work, place, outs, pieces=1):
    depth = outs[0].shape[0]
    start = pl.multiple_of(place * depth, depth)
    outs[0][...] = work[pl.ds(start, depth), :]
    piece = depth // pieces
    for index, out in enumerate(outs[1:]):
        start = (place ^ (index // pieces + 1)) * depth + (index % pieces) * piece
        out[...] = work[pl.ds(pl.multiple_of(start, piece), piece), :].astype(out.dtype)


def added(own_ref, terms):
    value = own_ref[...]
    for term in terms:
        value += term[...].astype(F32)
    return value


def share_body(size, apart, place_ref, *refs):
    ins, outs, works = refs[: -2 - size], refs[-2 - size : -2], refs[-2:]
    if apart:
        works[0][...] = added(ins[0], ins[1:2])
        works[1][...] = added(ins[2], ins[3:])
    else:
        value, split = added(ins[0], ins[1:]), works[0].shape[0]
        works[0][...] = value[:split]
        works[1][...] = value[split:]
    depths = [work.shape[0] // size for work in works]
    for step, out in enumerate(outs):
        parts = []
        for work, depth in zip(works, depths):
            start = pl.multiple_of((place_ref[0] ^ step) * depth, depth)
            parts.append(work[pl.ds(start, depth), :])
        out[...] = jnp.concatenate(parts, axis=0).astype(out.dtype)


def settle_body(own_ref, *refs):
    refs[-1][...] = added(own_ref, refs[:-1]).astype(BF16)


def finish_body(blocks, place_ref, own_ref, other_ref, update_ref, out_ref, in_ref):
    first = place_ref[0] == 0
    own, other = own_ref[...].astype(F32), other_ref[...].astype(F32)
    rows, hid = update_ref.shape[0], in_ref.shape[1]
    depth = own.shape[0] // blocks
    side = in_ref.shape[0] // (4 * blocks)
    split = depth - side
    for half in range(2):
        value = jnp.where(first, own, other) if half == 0 else jnp.where(first, other, own)
        for index in range(blocks):
            part = value[index * depth : (index + 1) * depth]
            start = (half * blocks + index) * split
            cut = min(max(rows - start, 0), split)
            if cut > 0:
                update_ref[start : start + cut, :] = part[:cut]
            if cut < split:
                out_ref[start + cut - rows : start + split - rows, :] = part[cut:split]
            start = (half * blocks + index) * side
            in_ref[start : start + side, :] = part[split:, :hid]
            start += in_ref.shape[0] // 2
            in_ref[start : start + side, :] = part[split:, hid:]


def backward_body(
    place_ref, grad_ref, far_counts_ref, far_slope_ref, far_table_ref, *refs
):
    far, near, sems = (far_counts_ref, far_slope_ref, far_table_ref), refs[-4:-1], refs[-1]
    copies = [pltpu.make_async_copy(a, b, sems.at[i]) for i, (a, b) in enumerate(zip(far, near))]
    for copy in copies:
        copy.start()
    counts_ref, slope_ref, table_t_ref = near
    grad = grad_ref[...]
    rows, work, refs = grad.shape[0], refs[-5], refs[:-5]
    copies[0].wait()
    both = dot(counts_ref[...], grad)
    copies[1].wait()
    high, low = halves((both[:rows] + 256.0 * both[rows:]) * slope_ref[...])
    copies[2].wait()
    table_t = table_t_ref[...]
    value = dot(table_t, high) + dot(table_t, low)
    half, hid = value.shape[0] // 2, value.shape[1]
    work[:, :hid] = value[:half]
    work[:, hid:] = value[half:]
    deal(work, place_ref[0], refs, len(refs) - 1)


def call(body, outs, args, scratch=(), flops=0, smem=0, limit=24, far=0):
    args = list(args)
    for index in range(len(args) - far, len(args)):
        args[index] = pltpu.with_memory_space_constraint(args[index], pltpu.HBM)
    outs = [jax.ShapeDtypeStruct(shape, kind) for shape, kind in outs]
    moved = sum(a.size * a.dtype.itemsize for a in list(args) + outs)
    vmem = pl.BlockSpec(memory_space=pltpu.VMEM)
    specs = [pl.BlockSpec(memory_space=pltpu.SMEM)] * smem + [vmem] * (len(args) - smem - far)
    specs += [pl.BlockSpec(memory_space=pl.ANY)] * far
    single = len(outs) == 1
    params = pltpu.CompilerParams(vmem_limit_bytes=limit << 20) if limit else None
    return pl.pallas_call(
        body,
        out_shape=outs[0] if single else outs,
        in_specs=specs,
        out_specs=vmem if single else [vmem] * len(outs),
        scratch_shapes=list(scratch),
        compiler_params=params,
        cost_estimate=pl.CostEstimate(
            flops=int(flops), bytes_accessed=int(moved), transcendentals=0
        ),
    )(*args)


PIECES = 1


class Cube:
    def __init__(self, n_group, n_dev, parts):
        self.total = n_group * n_dev
        self.size, self.steps, self.place = 1, [0], 0
        for axis, stride, size in parts:
            unit = stride * (n_dev if axis == "group" else 1)
            place = lax.rem(lax.div(lax.axis_index(axis), stride), size)
            self.place = self.place * size + place
            self.steps = [s | (i * unit) for s in self.steps for i in range(size)]
            self.size *= size

    def send(self, value, step):
        pairs = [(i, i ^ self.steps[step]) for i in range(self.total)]
        return lax.ppermute(value, ("group", "dev"), pairs)

    def scatter(self, value):
        blocks = value.reshape(self.size, -1, value.shape[1])
        own = lax.dynamic_index_in_dim(blocks, self.place, 0, False)
        terms = []
        for step in range(1, self.size):
            block = lax.dynamic_index_in_dim(blocks, self.place ^ step, 0, False)
            terms.append(self.send(block.astype(BF16), step))
        return own, terms

    def gather(self, value):
        parts = [value] + [self.send(value, step) for step in range(1, self.size)]
        bit = 1
        while bit < self.size:
            flip = (self.place & bit) > 0
            parts = [jnp.where(flip, parts[i ^ bit], parts[i]) for i in range(self.size)]
            bit *= 2
        return jnp.concatenate(parts, axis=0)


def total(own, terms):
    for term in terms:
        own += term.astype(F32)
    return own


def share(cube, depths, ins):
    apart = isinstance(ins[0], list)
    flat_ins = ins[0] + ins[1] if apart else ins
    width = flat_ins[0].shape[1]
    rows = [depth // cube.size for depth in depths]
    if any(count % 8 for count in rows):
        if apart:
            values = [total(group[0], group[1:]) for group in ins]
        else:
            values = jnp.split(total(ins[0], ins[1:]), [depths[0]], axis=0)
        values = [value.reshape(cube.size, -1, width) for value in values]
        return cube.scatter(jnp.concatenate(values, axis=1).reshape(-1, width))
    shape = (sum(rows), width)
    own, *sent = call(
        functools.partial(share_body, cube.size, apart),
        [(shape, F32)] + [(shape, BF16)] * (cube.size - 1),
        [cube.place.reshape(1), *flat_ins],
        scratch=[pltpu.VMEM((depth, width), F32) for depth in depths],
        smem=1,
    )
    return own, [cube.send(block, step + 1) for step, block in enumerate(sent)]


def shards(
    node_state,
    hub_state,
    w_edge_in,
    w_edge_out,
    w_update,
    edge_src,
    edge_dst,
    edge_mask,
    send_list,
    send_count,
    node_cot,
    hub_cot,
    *,
    n_group,
    n_dev,
):
    rows, width = node_state.shape
    hid = w_edge_in.shape[1]
    slots = send_list.shape[2]
    hubs = hub_state.shape[0]
    lay = Layout(n_dev, slots, hubs)
    both = ("group", "dev")
    run = functools.partial(call, limit=24 if lay.rows <= 512 else 48)
    def body(function, *static):
        return functools.partial(function, *static)

    packed = run(
        body(gather_body, lay),
        [((lay.rows, width), BF16)],
        [send_count, send_list[0], node_state, hub_state],
        smem=1,
        limit=None,
    )
    table = lax.all_to_all(packed, "dev", 0, 0, tiled=True)

    square = ((lay.rows, lay.rows), BF16)
    edges = [edge_src, edge_dst, edge_mask]
    low, high, count_rows, near, wide = run(
        body(count_body, lay),
        [
            square,
            square,
            ((lay.wide_rows, hid), BF16),
            ((1, lay.rows), I32),
            ((1, lay.wide_rows), I32),
        ],
        [send_count, send_list[0]] + edges,
        scratch=[pltpu.VMEM((lay.rows, lay.rows), F32)],
        flops=2 * edge_src.shape[0] * lay.rows * lay.rows,
        smem=1,
    )
    message = run(
        body(forward_body, lay),
        [((lay.wide_rows, hid), BF16)],
        [table, w_edge_in, low, high, count_rows],
    )
    back = lax.all_to_all(message, "dev", 0, 0, tiled=True)
    turned = run(
        slope_body,
        [((lay.rows, hid), F32), ((width, lay.rows), BF16), ((2 * lay.rows, lay.rows), BF16)],
        [table, w_edge_in, low, high],
        flops=2 * lay.rows * width * hid,
    )
    back, (slope, table_t, counts_t) = lax.optimization_barrier((back, turned))

    hub_part = run(body(hub_sum_body, lay), [((hubs, hid + 128), F32)], [back])
    group_cube = Cube(n_group, n_dev, [("group", 1, n_group)])
    parts = [hub_part] + [group_cube.send(hub_part, step) for step in range(1, n_group)]

    def row_outs(count):
        return [
            ((count, width), BF16),
            ((count, width), BF16),
            ((count, width), BF16),
            ((count, hid), BF16),
            ((count, hid), BF16),
            ((count, width), BF16),
        ]

    far = [node_state, node_cot, w_edge_out, w_update, hub_state, hub_cot]
    master = run(
        body(master_body, lay, len(far)),
        row_outs(rows) + [((lay.rows, hid), F32)] + [(a.shape, a.dtype) for a in far[2:]],
        [near, wide, back] + far,
        scratch=[
            pltpu.VMEM((rows, width), BF16),
            pltpu.VMEM((rows, width), BF16),
            pltpu.SemaphoreType.DMA((len(far),)),
        ],
        flops=2 * rows * (2 * lay.rows * hid + 2 * width * width + 2 * width * hid),
        far=len(far),
    )
    new_state, saved, grad_rows = master[0], list(master[1:6]), master[6]
    w_out, w_up, hub_rows, hub_grads = master[7:]
    new_hub, *hub_saved, grad_message = run(
        body(hub_body, lay, n_group),
        row_outs(hubs) + [((lay.rows, hid), BF16)],
        parts + [hub_rows, hub_grads, w_out, w_up, grad_rows],
    )
    grad_table = lax.all_to_all(grad_message, "dev", 0, 0, tiled=True)

    core = Cube(n_group, n_dev, [("group", 1, 2)])
    flat = Cube(n_group, n_dev, [("group", 2, n_group // 2), ("dev", 1, 2)])
    line = Cube(n_group, n_dev, [("dev", 2, n_dev // 2)])
    upper_rows = width + hid

    half, quarter = upper_rows // 2, width // 4
    first = (lax.axis_index("group") == 0).astype(I32)
    own, *sent = run(
        weight_body,
        [((half, width), F32)] + [((half // PIECES, width), BF16)] * PIECES,
        [jnp.stack([first, core.place])] + saved + hub_saved,
        scratch=[pltpu.VMEM((upper_rows, width), F32)],
        flops=2 * rows * width * (width + 2 * hid),
        smem=1,
    )
    upper = [own] + [core.send(block, 1) for block in sent]
    side, *sent = run(
        backward_body,
        [((quarter, width), F32)] + [((quarter // PIECES, width), BF16)] * PIECES,
        [core.place.reshape(1), grad_table, counts_t, slope, table_t],
        scratch=[
            pltpu.VMEM((width // 2, width), F32),
            pltpu.VMEM(counts_t.shape, BF16),
            pltpu.VMEM(slope.shape, F32),
            pltpu.VMEM(table_t.shape, BF16),
            pltpu.SemaphoreType.DMA((3,)),
        ],
        far=3,
        flops=2 * lay.rows * hid * (lay.rows + width) * 2,
        smem=1,
    )
    side = [side] + [core.send(block, 1) for block in sent]
    depths = [half, quarter]
    for cube in (flat, line):
        own, terms = share(cube, depths, [upper, side] if cube is flat else [own, *terms])
        depths = [depth // cube.size for depth in depths]
    block = sum(depths)
    if depths[1] % 8 == 0:
        whole = run(settle_body, [((block, width), BF16)], [own, *terms])
    else:
        whole = total(own, terms).astype(BF16)
    for cube in (line, flat):
        whole = cube.gather(whole)
    if depths[1] % 8 == 0:
        grad_update, grad_out, grad_in = run(
            body(finish_body, n_group * n_dev // 2),
            [((width, width), F32), ((hid, width), F32), ((width, hid), F32)],
            [core.place.reshape(1), whole, core.send(whole, 1)],
            smem=1,
        )
        return new_state, new_hub, grad_in, grad_out, grad_update
    whole = core.gather(whole).reshape(n_group * n_dev, -1, width).astype(F32)
    upper = whole[:, : depths[0]].reshape(-1, width)
    side = whole[:, depths[0] :].reshape(-1, width)
    side = jnp.concatenate([side[:, :hid], side[:, hid:]], axis=0)
    return new_state, new_hub, side, upper[width:], upper[:width]


def solution(mesh):
    def body(*args):
        return shards(*args, n_group=mesh.shape["group"], n_dev=mesh.shape["dev"])

    return jax.shard_map(
        body,
        mesh=mesh,
        in_specs=(
            P(("group", "dev"), None),
            P("dev", None),
            P(),
            P(),
            P(),
            P(("group", "dev")),
            P(("group", "dev")),
            P(("group", "dev")),
            P(("group", "dev"), None, None),
            P(("group", "dev"), None),
            P(("group", "dev"), None),
            P("dev", None),
        ),
        out_specs=(P(("group", "dev"), None), P("dev", None), P(), P(), P()),
        check_vma=False,
    )
```

time: 97 us -> 91 us (0.938)
  Pallas kernels: 12 us -> 19 us
  local copies, waits for them, and re-layouts: 7.7 us -> 2.28 us
  starting transfers between devices: 36.3 us -> 32.7 us
  other arithmetic: 3.27 us -> 0.32 us
    pallas_call x9 -> x13, Pallas kernels: 12 us -> 19 us  [call(): pl.pallas_call(body, out_shape=outs[0] if single else outs, in_specs=spec...]
    all_to_all x1 -> x0, starting transfers between devices: 3.7 us -> none  [shards(): side = lax.all_to_all(side, both, 0, 0, tiled=True)]
    all_to_all x1, waiting for transfers between devices: 7.81 us -> 4.61 us  [shards(): back = lax.all_to_all(message, 'dev', 0, 0, tiled=True)]
    unnamed x28 -> x18, local copies, waits for them, and re-layouts: 4.64 us -> 2.28 us
    slice x5 -> x0, local copies, waits for them, and re-layouts: 2.09 us -> none  [the longest x2 1.87 us: shards(): return (new_state, new_hub, side, upper[width:], upper[:width])]
    all_to_all x1, waiting for transfers between devices: 3.37 us -> 5.44 us  [shards(): grad_table = lax.all_to_all(grad_message, 'dev', 0, 0, tiled=True)]
    ppermute x17 -> x18, waiting for transfers between devices: 15.8 us -> 17.8 us  [send(): return lax.ppermute(value, ('group', 'dev'), pairs)]
    all_to_all x1, waiting for transfers between devices: 9.24 us -> 7.4 us  [shards(): table = lax.all_to_all(packed, 'dev', 0, 0, tiled=True)]
  transfers between devices with their start and end apart: 21 -> 21, of which waited for: 12 -> 14; matrix products, arithmetic and copies ran while one was open for 1% -> 0% of each run, Pallas kernels for 7% -> 14%
where the time goes in v3:
time: 91 us; the launch traced here: 90.4 us
  waiting for transfers between devices  35.3 us (39%)
  starting transfers between devices  32.7 us (36%)
  Pallas kernels  19 us (21%)
  local copies, waits for them, and re-layouts  2.28 us (3%)
    pallas_call x13, Pallas kernels, call(): pl.pallas_call(body, out_shape=outs[0] if single else outs, in_specs=spec...  19 us
    ppermute x18, starting transfers between devices, send(): return lax.ppermute(value, ('group', 'dev'), pairs)  18.4 us
    ppermute x18, waiting for transfers between devices, send(): return lax.ppermute(value, ('group', 'dev'), pairs)  17.8 us
    all_to_all x1, waiting for transfers between devices, shards(): table = lax.all_to_all(packed, 'dev', 0, 0, tiled=True)  7.4 us
    all_to_all x1, starting transfers between devices, shards(): table = lax.all_to_all(packed, 'dev', 0, 0, tiled=True)  7.4 us
    all_to_all x1, waiting for transfers between devices, shards(): grad_table = lax.all_to_all(grad_message, 'dev', 0, 0, tiled=True)  5.44 us
    all_to_all x1, waiting for transfers between devices, shards(): back = lax.all_to_all(message, 'dev', 0, 0, tiled=True)  4.61 us
    all_to_all x1, starting transfers between devices, shards(): back = lax.all_to_all(message, 'dev', 0, 0, tiled=True)  3.59 us
  transfers between devices with their start and end apart: 21, of which 14 were waited for; matrix products, arithmetic and copies ran while one was open for 0% of the time, Pallas kernels for 14%

profile of v3, /device:TPU:0, one launch (start us, length us, event | category | flops | bytes accessed | tf_op | source)
XLA Modules:
  0.0 90.4 jit_solution(12811552778494430366)
XLA Ops:
  0.6 2.3 %shard_map.156 = bf16[320,512]{1,0:T(8,128)(2,1)} custom-call(s32[1,8]{1,0:T(1,128)} %count_ref.3, s32[8,32]{1,0:T(8,128)} %bitcast.16, bf16[512,512]{1,0:T(8,128)(2,1)} %refs_0_.1, bf16[8,512]{1,0:T(8,128)(2,1)} %refs_4_.1), custom_call_target="tpu_custom_call" | custom-call | bytes 861216 | tf_op jit(solution)/shard_map/pallas_call | solution.py:375
  2.9 7.4 %all-to-all-start = ((bf16[8,40,512]{2,1,0:T(8,128)(2,1)}), bf16[8,40,512]{2,1,0:T(8,128)(2,1)S(1)}, u32[]{:S(2)}, u32[]{:S(2)}) async-start(bf16[8,40,512]{2,1,0:T(8,128)(2,1)} %bitcast.18), calls=%async_computation | async-start | bytes 655360 | tf_op jit(solution)/shard_map/all_to_all | solution.py:488
  10.4 2.9 %shard_map.155 = (bf16[320,320]{1,0:T(8,128)(2,1)S(1)}, bf16[320,320]{1,0:T(8,128)(2,1)S(1)}, bf16[384,256]{1,0:T(8,128)(2,1)S(1)}, s32[1,320]{1,0:T(1,128)S(1)}, s32[1,384]{1,0:T(1,128)S(1)}) custom-call(s32[1,8]{1,0:T(1,128)S(1)} %copy-done.5, s32[8,32]{1,0:T(8,128)S(1)} %bitcast.17, s32[4096]{0:T(1024)S(1)} %copy-done.6, s32[4096]{0:T(1024)S(1)} %copy-done.7, ...), custom_call_target="tpu_custom_call" | custom-call | flops 838860800 | bytes 659232 | tf_op jit(solution)/shard_map/pallas_call | solution.py:375
  13.3 7.4 %all-to-all-done = bf16[8,40,512]{2,1,0:T(8,128)(2,1)S(1)} async-done(((bf16[8,40,512]{2,1,0:T(8,128)(2,1)}), bf16[8,40,512]{2,1,0:T(8,128)(2,1)S(1)}, u32[]{:S(2)}, u32[]{:S(2)}) %all-to-all-start) | async-done | bytes 327712 | tf_op jit(solution)/shard_map/all_to_all | solution.py:488
  21.9 3.6 %all-to-all-start.1 = ((bf16[8,48,256]{2,1,0:T(8,128)(2,1)}), bf16[8,48,256]{2,1,0:T(8,128)(2,1)S(1)}, u32[]{:S(2)}, u32[]{:S(2)}) async-start(bf16[8,48,256]{2,1,0:T(8,128)(2,1)} %bitcast.3), calls=%async_computation.1 | async-start | bytes 393216 | tf_op jit(solution)/shard_map/all_to_all | solution.py:511
  28.6 4.6 %all-to-all-done.1 = bf16[8,48,256]{2,1,0:T(8,128)(2,1)S(1)} async-done(((bf16[8,48,256]{2,1,0:T(8,128)(2,1)}), bf16[8,48,256]{2,1,0:T(8,128)(2,1)S(1)}, u32[]{:S(2)}, u32[]{:S(2)}) %all-to-all-start.1) | async-done | bytes 196640 | tf_op jit(solution)/shard_map/all_to_all | solution.py:511
  33.4 1.6 %collective-permute-start.1 = (f32[8,384]{1,0:T(8,128)S(1)}, f32[8,384]{1,0:T(8,128)S(1)}, u32[]{:S(2)}, u32[]{:S(2)}) collective-permute-start(f32[8,384]{1,0:T(8,128)S(1)} %shard_map.160.refs_0_), channel_id=1, source_target_pairs={{0,16},{1,17},{2,18},{3,19},{4,20},{5,21},{6,22},{7,23},{8,24},{9,... | collective-permute-start | bytes 36872 | tf_op jit(solution)/shard_map/ppermute | solution.py:404
  35.2 4.0 %shard_map.159 = (bf16[512,512]{1,0:T(8,128)(2,1)}, bf16[512,512]{1,0:T(8,128)(2,1)S(1)}, bf16[512,512]{1,0:T(8,128)(2,1)S(1)}, bf16[512,256]{1,0:T(8,128)(2,1)S...) custom-call(s32[1,320]{1,0:T(1,128)S(1)} %get-tuple-element.50.near_, ...), custom_call_target="tpu_custom_call" | custom-call | flops 973078528 | bytes 5802752 | tf_op jit(solution)/shard_map/pallas_call | solution.py:375
  39.2 1.4 %shard_map.161 = (bf16[8,512]{1,0:T(8,128)(2,1)}, bf16[8,512]{1,0:T(8,128)(2,1)S(1)}, bf16[8,512]{1,0:T(8,128)(2,1)S(1)}, bf16[8,256]{1,0:T(8,128)(2,1)S(1)}, bf...) custom-call(f32[8,384]{1,0:T(8,128)S(1)} %shard_map.160.refs_0_, ...), custom_call_target="tpu_custom_call" | custom-call | bytes 1384448 | tf_op jit(solution)/shard_map/pallas_call | solution.py:375
  40.6 3.4 %all-to-all-start.2 = ((bf16[8,40,256]{2,1,0:T(8,128)(2,1)}), bf16[8,40,256]{2,1,0:T(8,128)(2,1)S(1)}, u32[]{:S(2)}, u32[]{:S(2)}) async-start(bf16[8,40,256]{2,1,0:T(8,128)(2,1)} %bitcast.9), calls=%async_computation.2 | async-start | bytes 327680 | tf_op jit(solution)/shard_map/all_to_all | solution.py:554
  44.0 2.4 %shard_map.162 = (f32[384,512]{1,0:T(8,128)S(1)}, bf16[384,512]{1,0:T(8,128)(2,1)}) custom-call(s32[2]{0:T(128)S(1)} %pad_add_fusion.place_ref, bf16[512,512]{1,0:T(8,128)(2,1)S(1)} %get-tuple-element.66.mixed_ref, bf16[512,512]{1,0:T(8,128)(2,1)S(1)} %get-tuple-element.67.pre_ref, bf16[512,256]{1,0:T(8,128)(2,1)S(1)} %get-tuple-element.68.high_ref, ...), custom_call_target="tpu_custom_call" | custom-call | flops 536870912 | bytes 3309576 | tf_op jit(solution)/shard_map/pallas_call | solution.py:375
  46.8 5.4 %all-to-all-done.2 = bf16[8,40,256]{2,1,0:T(8,128)(2,1)S(1)} async-done(((bf16[8,40,256]{2,1,0:T(8,128)(2,1)}), bf16[8,40,256]{2,1,0:T(8,128)(2,1)S(1)}, u32[]{:S(2)}, u32[]{:S(2)}) %all-to-all-start.2) | async-done | bytes 163872 | tf_op jit(solution)/shard_map/all_to_all | solution.py:554
  52.2 2.3 %shard_map.163 = (f32[128,512]{1,0:T(8,128)S(1)}, bf16[128,512]{1,0:T(8,128)(2,1)S(1)}) custom-call(s32[1]{0:T(128)} %bitcast.5.place_ref, bf16[320,256]{1,0:T(8,128)(2,1)S(1)} %bitcast.15, bf16[640,320]{1,0:T(8,128)(2,1)} %copy-done.1, f32[320,256]{1,0:T(8,128)} %copy-done.3, bf16[512,320]{1,0:T(8,128)(2,1)} %copy-done.2), custom_call_target="tpu_custom_call" | custom-call | flops 272629760 | bytes 1622020 | tf_op jit(solution)/shard_map/pallas_call | solution.py:375
  56.5 1.5 %collective-permute-start.6 = (bf16[128,512]{1,0:T(8,128)(2,1)S(1)}, bf16[128,512]{1,0:T(8,128)(2,1)S(1)}, u32[]{:S(2)}, u32[]{:S(2)}) collective-permute-start(bf16[128,512]{1,0:T(8,128)(2,1)S(1)} %get-tuple-element.86), channel_id=1, source_target_pairs={{0,16},{1,17},{2,18},{3,19},{4,20},{5,21},{6,22},{7,23},{8,24},{9,... | collective-permute-start | bytes 393224 | tf_op jit(solution)/shard_map/ppermute | solution.py:404
  58.0 1.7 %collective-permute-start.7 = (bf16[128,512]{1,0:T(8,128)(2,1)S(1)}, bf16[128,512]{1,0:T(8,128)(2,1)S(1)}, u32[]{:S(2)}, u32[]{:S(2)}) collective-permute-start(bf16[128,512]{1,0:T(8,128)(2,1)S(1)} %get-tuple-element.87), channel_id=1, source_target_pairs={{0,17},{1,16},{2,19},{3,18},{4,21},{5,20},{6,23},{7,22},{8,25},{9,... | collective-permute-start | bytes 393224 | tf_op jit(solution)/shard_map/ppermute | solution.py:404
  59.6 2.9 %collective-permute-done.5.refs_1_ = bf16[128,512]{1,0:T(8,128)(2,1)S(1)} collective-permute-done((bf16[128,512]{1,0:T(8,128)(2,1)S(1)}, bf16[128,512]{1,0:T(8,128)(2,1)S(1)}, u32[]{:S(2)}, u32[]{:S(2)}) %collective-permute-start.5) | collective-permute-done | bytes 131104 | tf_op jit(solution)/shard_map/ppermute | solution.py:404
  62.5 3.0 %collective-permute-done.7.refs_3_ = bf16[128,512]{1,0:T(8,128)(2,1)S(1)} collective-permute-done((bf16[128,512]{1,0:T(8,128)(2,1)S(1)}, bf16[128,512]{1,0:T(8,128)(2,1)S(1)}, u32[]{:S(2)}, u32[]{:S(2)}) %collective-permute-start.7) | collective-permute-done | bytes 131104 | tf_op jit(solution)/shard_map/ppermute | solution.py:404
  66.7 3.3 %collective-permute-start.9 = (bf16[32,512]{1,0:T(8,128)(2,1)S(1)}, bf16[32,512]{1,0:T(8,128)(2,1)S(1)}, u32[]{:S(2)}, u32[]{:S(2)}) collective-permute-start(bf16[32,512]{1,0:T(8,128)(2,1)S(1)} %get-tuple-element.90), channel_id=1, source_target_pairs={{0,4},{1,5},{2,6},{3,7},{4,0},{5,1},{6,2},{7,3},{8,12},{9,13},{10,... | collective-permute-start | bytes 98312 | tf_op jit(solution)/shard_map/ppermute | solution.py:404
  71.9 2.4 %collective-permute-start.11 = (bf16[32,512]{1,0:T(8,128)(2,1)S(1)}, bf16[32,512]{1,0:T(8,128)(2,1)S(1)}, u32[]{:S(2)}, u32[]{:S(2)}) collective-permute-start(bf16[32,512]{1,0:T(8,128)(2,1)S(1)} %shard_map.166), channel_id=1, source_target_pairs={{0,6},{1,7},{2,4},{3,5},{4,2},{5,3},{6,0},{7,1},{8,14},{9,15},{10,... | collective-permute-start | bytes 98312 | tf_op jit(solution)/shard_map/ppermute | solution.py:404
  75.0 1.4 %collective-permute-start.13 = (bf16[32,512]{1,0:T(8,128)(2,1)S(1)}, bf16[32,512]{1,0:T(8,128)(2,1)S(1)}, u32[]{:S(2)}, u32[]{:S(2)}) collective-permute-start(bf16[32,512]{1,0:T(8,128)(2,1)S(1)} %shard_map.166), channel_id=1, source_target_pairs={{0,2},{1,3},{2,0},{3,1},{4,6},{5,7},{6,4},{7,5},{8,10},{9,11},{10,... | collective-permute-start | bytes 98312 | tf_op jit(solution)/shard_map/ppermute | solution.py:404
  77.7 1.6 %collective-permute-done.12 = bf16[32,512]{1,0:T(8,128)(2,1)S(1)} collective-permute-done((bf16[32,512]{1,0:T(8,128)(2,1)S(1)}, bf16[32,512]{1,0:T(8,128)(2,1)S(1)}, u32[]{:S(2)}, u32[]{:S(2)}) %collective-permute-start.12) | collective-permute-done | bytes 32800 | tf_op jit(solution)/shard_map/ppermute | solution.py:404
  79.3 1.8 %collective-permute-start.14 = (bf16[128,512]{1,0:T(8,128)(2,1)S(1)}, bf16[128,512]{1,0:T(8,128)(2,1)S(1)}, u32[]{:S(2)}, u32[]{:S(2)}) collective-permute-start(bf16[128,512]{1,0:T(8,128)(2,1)S(1)} %pad_maximum_fusion.1), channel_id=1, source_target_pairs={{0,17},{1,16},{2,19},{3,18},{4,21},{5,20},{6,23},{7,22},{8,25},{9,... | collective-permute-start | bytes 393224 | tf_op jit(solution)/shard_map/ppermute | solution.py:404
  82.8 2.4 %collective-permute-done.14 = bf16[128,512]{1,0:T(8,128)(2,1)S(1)} collective-permute-done((bf16[128,512]{1,0:T(8,128)(2,1)S(1)}, bf16[128,512]{1,0:T(8,128)(2,1)S(1)}, u32[]{:S(2)}, u32[]{:S(2)}) %collective-permute-start.14) | collective-permute-done | bytes 131104 | tf_op jit(solution)/shard_map/ppermute | solution.py:404
  87.1 1.9 %collective-permute-done.17.other_ref = bf16[512,512]{1,0:T(8,128)(2,1)S(1)} collective-permute-done((bf16[512,512]{1,0:T(8,128)(2,1)S(1)}, bf16[512,512]{1,0:T(8,128)(2,1)S(1)}, u32[]{:S(2)}, u32[]{:S(2)}) %collective-permute-start.17) | collective-permute-done | bytes 524320 | tf_op jit(solution)/shard_map/ppermute | solution.py:404
  (55 shorter events, 17.1 us)
Async XLA Ops:
  2.9 7.4 %copy-start.7 = (s32[4096]{0:T(1024)S(1)}, s32[4096]{0:T(1024)}, u32[]{:S(2)}) copy-start(s32[4096]{0:T(1024)} %dst_ref.1) | copy-start | bytes 49156
  2.9 7.4 %copy-start.8 = (s32[4096]{0:T(1024)S(1)}, s32[4096]{0:T(1024)}, u32[]{:S(2)}) copy-start(s32[4096]{0:T(1024)} %mask_ref.1) | copy-start | bytes 49156
  2.9 17.7 %all-to-all-start = ((bf16[8,40,512]{2,1,0:T(8,128)(2,1)}), bf16[8,40,512]{2,1,0:T(8,128)(2,1)S(1)}, u32[]{:S(2)}, u32[]{:S(2)}) async-start(bf16[8,40,512]{2,1,0:T(8,128)(2,1)} %bitcast.18), calls=%async_computation | async-start | bytes 655360 | tf_op jit(solution)/shard_map/all_to_all | solution.py:488
  10.4 10.3 %copy-start = (bf16[512,256]{1,0:T(8,128)(2,1)S(1)}, bf16[512,256]{1,0:T(8,128)(2,1)}, u32[]{:S(2)}) copy-start(bf16[512,256]{1,0:T(8,128)(2,1)} %w_ref.3) | copy-start | bytes 786436
  21.9 11.4 %all-to-all-start.1 = ((bf16[8,48,256]{2,1,0:T(8,128)(2,1)}), bf16[8,48,256]{2,1,0:T(8,128)(2,1)S(1)}, u32[]{:S(2)}, u32[]{:S(2)}) async-start(bf16[8,48,256]{2,1,0:T(8,128)(2,1)} %bitcast.3), calls=%async_computation.1 | async-start | bytes 393216 | tf_op jit(solution)/shard_map/all_to_all | solution.py:511
  33.4 5.9 %collective-permute-start = (f32[8,384]{1,0:T(8,128)S(1)}, f32[8,384]{1,0:T(8,128)S(1)}, u32[]{:S(2)}, u32[]{:S(2)}) collective-permute-start(f32[8,384]{1,0:T(8,128)S(1)} %shard_map.160.refs_0_), channel_id=1, source_target_pairs={{0,8},{1,9},{2,10},{3,11},{4,12},{5,13},{6,14},{7,15},{8,0},{9,1},... | collective-permute-start | bytes 36872 | tf_op jit(solution)/shard_map/ppermute | solution.py:404
  33.4 5.9 %collective-permute-start.1 = (f32[8,384]{1,0:T(8,128)S(1)}, f32[8,384]{1,0:T(8,128)S(1)}, u32[]{:S(2)}, u32[]{:S(2)}) collective-permute-start(f32[8,384]{1,0:T(8,128)S(1)} %shard_map.160.refs_0_), channel_id=1, source_target_pairs={{0,16},{1,17},{2,18},{3,19},{4,20},{5,21},{6,22},{7,23},{8,24},{9,... | collective-permute-start | bytes 36872 | tf_op jit(solution)/shard_map/ppermute | solution.py:404
  34.9 4.3 %collective-permute-start.2 = (f32[8,384]{1,0:T(8,128)S(1)}, f32[8,384]{1,0:T(8,128)S(1)}, u32[]{:S(2)}, u32[]{:S(2)}) collective-permute-start(f32[8,384]{1,0:T(8,128)S(1)} %shard_map.160.refs_0_), channel_id=1, source_target_pairs={{0,24},{1,25},{2,26},{3,27},{4,28},{5,29},{6,30},{7,31},{8,16},{9,... | collective-permute-start | bytes 36872 | tf_op jit(solution)/shard_map/ppermute | solution.py:404
  40.6 11.6 %all-to-all-start.2 = ((bf16[8,40,256]{2,1,0:T(8,128)(2,1)}), bf16[8,40,256]{2,1,0:T(8,128)(2,1)S(1)}, u32[]{:S(2)}, u32[]{:S(2)}) async-start(bf16[8,40,256]{2,1,0:T(8,128)(2,1)} %bitcast.9), calls=%async_computation.2 | async-start | bytes 327680 | tf_op jit(solution)/shard_map/all_to_all | solution.py:554
  46.4 8.2 %collective-permute-start.3 = (bf16[384,512]{1,0:T(8,128)(2,1)}, bf16[384,512]{1,0:T(8,128)(2,1)S(1)}, u32[]{:S(2)}, u32[]{:S(2)}) collective-permute-start(bf16[384,512]{1,0:T(8,128)(2,1)} %get-tuple-element.77), channel_id=1, source_target_pairs={{0,8},{1,9},{2,10},{3,11},{4,12},{5,13},{6,14},{7,15},{8,0},{9,1},... | collective-permute-start | bytes 1179656 | tf_op jit(solution)/shard_map/ppermute | solution.py:404
  54.5 1.4 %collective-permute-start.4 = (bf16[128,512]{1,0:T(8,128)(2,1)S(1)}, bf16[128,512]{1,0:T(8,128)(2,1)S(1)}, u32[]{:S(2)}, u32[]{:S(2)}) collective-permute-start(bf16[128,512]{1,0:T(8,128)(2,1)S(1)} %get-tuple-element.83), channel_id=1, source_target_pairs={{0,8},{1,9},{2,10},{3,11},{4,12},{5,13},{6,14},{7,15},{8,0},{9,1},... | collective-permute-start | bytes 393224 | tf_op jit(solution)/shard_map/ppermute | solution.py:404
  56.1 6.4 %collective-permute-start.5 = (bf16[128,512]{1,0:T(8,128)(2,1)S(1)}, bf16[128,512]{1,0:T(8,128)(2,1)S(1)}, u32[]{:S(2)}, u32[]{:S(2)}) collective-permute-start(bf16[128,512]{1,0:T(8,128)(2,1)S(1)} %get-tuple-element.85), channel_id=1, source_target_pairs={{0,1},{1,0},{2,3},{3,2},{4,5},{5,4},{6,7},{7,6},{8,9},{9,8},{10,11... | collective-permute-start | bytes 393224 | tf_op jit(solution)/shard_map/ppermute | solution.py:404
  56.5 6.0 %collective-permute-start.6 = (bf16[128,512]{1,0:T(8,128)(2,1)S(1)}, bf16[128,512]{1,0:T(8,128)(2,1)S(1)}, u32[]{:S(2)}, u32[]{:S(2)}) collective-permute-start(bf16[128,512]{1,0:T(8,128)(2,1)S(1)} %get-tuple-element.86), channel_id=1, source_target_pairs={{0,16},{1,17},{2,18},{3,19},{4,20},{5,21},{6,22},{7,23},{8,24},{9,... | collective-permute-start | bytes 393224 | tf_op jit(solution)/shard_map/ppermute | solution.py:404
  58.0 7.5 %collective-permute-start.7 = (bf16[128,512]{1,0:T(8,128)(2,1)S(1)}, bf16[128,512]{1,0:T(8,128)(2,1)S(1)}, u32[]{:S(2)}, u32[]{:S(2)}) collective-permute-start(bf16[128,512]{1,0:T(8,128)(2,1)S(1)} %get-tuple-element.87), channel_id=1, source_target_pairs={{0,17},{1,16},{2,19},{3,18},{4,21},{5,20},{6,23},{7,22},{8,25},{9,... | collective-permute-start | bytes 393224 | tf_op jit(solution)/shard_map/ppermute | solution.py:404
  65.5 5.8 %collective-permute-start.10 = (bf16[32,512]{1,0:T(8,128)(2,1)S(1)}, bf16[32,512]{1,0:T(8,128)(2,1)S(1)}, u32[]{:S(2)}, u32[]{:S(2)}) collective-permute-start(bf16[32,512]{1,0:T(8,128)(2,1)S(1)} %get-tuple-element.91), channel_id=1, source_target_pairs={{0,6},{1,7},{2,4},{3,5},{4,2},{5,3},{6,0},{7,1},{8,14},{9,15},{10,... | collective-permute-start | bytes 98312 | tf_op jit(solution)/shard_map/ppermute | solution.py:404
  66.6 4.8 %collective-permute-start.8 = (bf16[32,512]{1,0:T(8,128)(2,1)S(1)}, bf16[32,512]{1,0:T(8,128)(2,1)S(1)}, u32[]{:S(2)}, u32[]{:S(2)}) collective-permute-start(bf16[32,512]{1,0:T(8,128)(2,1)S(1)} %get-tuple-element.89), channel_id=1, source_target_pairs={{0,2},{1,3},{2,0},{3,1},{4,6},{5,7},{6,4},{7,5},{8,10},{9,11},{10,... | collective-permute-start | bytes 98312 | tf_op jit(solution)/shard_map/ppermute | solution.py:404
  66.7 5.2 %collective-permute-start.9 = (bf16[32,512]{1,0:T(8,128)(2,1)S(1)}, bf16[32,512]{1,0:T(8,128)(2,1)S(1)}, u32[]{:S(2)}, u32[]{:S(2)}) collective-permute-start(bf16[32,512]{1,0:T(8,128)(2,1)S(1)} %get-tuple-element.90), channel_id=1, source_target_pairs={{0,4},{1,5},{2,6},{3,7},{4,0},{5,1},{6,2},{7,3},{8,12},{9,13},{10,... | collective-permute-start | bytes 98312 | tf_op jit(solution)/shard_map/ppermute | solution.py:404
  71.9 5.8 %collective-permute-start.11 = (bf16[32,512]{1,0:T(8,128)(2,1)S(1)}, bf16[32,512]{1,0:T(8,128)(2,1)S(1)}, u32[]{:S(2)}, u32[]{:S(2)}) collective-permute-start(bf16[32,512]{1,0:T(8,128)(2,1)S(1)} %shard_map.166), channel_id=1, source_target_pairs={{0,6},{1,7},{2,4},{3,5},{4,2},{5,3},{6,0},{7,1},{8,14},{9,15},{10,... | collective-permute-start | bytes 98312 | tf_op jit(solution)/shard_map/ppermute | solution.py:404
  74.3 4.9 %collective-permute-start.12 = (bf16[32,512]{1,0:T(8,128)(2,1)S(1)}, bf16[32,512]{1,0:T(8,128)(2,1)S(1)}, u32[]{:S(2)}, u32[]{:S(2)}) collective-permute-start(bf16[32,512]{1,0:T(8,128)(2,1)S(1)} %shard_map.166), channel_id=1, source_target_pairs={{0,4},{1,5},{2,6},{3,7},{4,0},{5,1},{6,2},{7,3},{8,12},{9,13},{10,... | collective-permute-start | bytes 98312 | tf_op jit(solution)/shard_map/ppermute | solution.py:404
  75.0 4.3 %collective-permute-start.13 = (bf16[32,512]{1,0:T(8,128)(2,1)S(1)}, bf16[32,512]{1,0:T(8,128)(2,1)S(1)}, u32[]{:S(2)}, u32[]{:S(2)}) collective-permute-start(bf16[32,512]{1,0:T(8,128)(2,1)S(1)} %shard_map.166), channel_id=1, source_target_pairs={{0,2},{1,3},{2,0},{3,1},{4,6},{5,7},{6,4},{7,5},{8,10},{9,11},{10,... | collective-permute-start | bytes 98312 | tf_op jit(solution)/shard_map/ppermute | solution.py:404
  79.3 6.0 %collective-permute-start.14 = (bf16[128,512]{1,0:T(8,128)(2,1)S(1)}, bf16[128,512]{1,0:T(8,128)(2,1)S(1)}, u32[]{:S(2)}, u32[]{:S(2)}) collective-permute-start(bf16[128,512]{1,0:T(8,128)(2,1)S(1)} %pad_maximum_fusion.1), channel_id=1, source_target_pairs={{0,17},{1,16},{2,19},{3,18},{4,21},{5,20},{6,23},{7,22},{8,25},{9,... | collective-permute-start | bytes 393224 | tf_op jit(solution)/shard_map/ppermute | solution.py:404
  81.1 5.5 %collective-permute-start.15 = (bf16[128,512]{1,0:T(8,128)(2,1)S(1)}, bf16[128,512]{1,0:T(8,128)(2,1)S(1)}, u32[]{:S(2)}, u32[]{:S(2)}) collective-permute-start(bf16[128,512]{1,0:T(8,128)(2,1)S(1)} %pad_maximum_fusion.1), channel_id=1, source_target_pairs={{0,16},{1,17},{2,18},{3,19},{4,20},{5,21},{6,22},{7,23},{8,24},{9,... | collective-permute-start | bytes 393224 | tf_op jit(solution)/shard_map/ppermute | solution.py:404
  81.9 5.0 %collective-permute-start.16 = (bf16[128,512]{1,0:T(8,128)(2,1)S(1)}, bf16[128,512]{1,0:T(8,128)(2,1)S(1)}, u32[]{:S(2)}, u32[]{:S(2)}) collective-permute-start(bf16[128,512]{1,0:T(8,128)(2,1)S(1)} %pad_maximum_fusion.1), channel_id=1, source_target_pairs={{0,1},{1,0},{2,3},{3,2},{4,5},{5,4},{6,7},{7,6},{8,9},{9,8},{10,11... | collective-permute-start | bytes 393224 | tf_op jit(solution)/shard_map/ppermute | solution.py:404
  87.1 2.0 %collective-permute-start.17 = (bf16[512,512]{1,0:T(8,128)(2,1)S(1)}, bf16[512,512]{1,0:T(8,128)(2,1)S(1)}, u32[]{:S(2)}, u32[]{:S(2)}) collective-permute-start(bf16[512,512]{1,0:T(8,128)(2,1)S(1)} %pad_maximum_fusion.own_ref), channel_id=1, source_target_pairs={{0,8},{1,9},{2,10},{3,11},{4,12},{5,13},{6,14},{7,15},{8,0},{9,1},... | collective-permute-start | bytes 1572872 | tf_op jit(solution)/shard_map/ppermute | solution.py:404
  (6 other events, 24.6 us)

commit v4 on v3

--- a/solution.py
+++ b/solution.py
@@ -172,17 +172,24 @@
     share = 1.0 / jnp.maximum(degree, 1.0)
     mixed = (states + (dot(high, w_out) + dot(low, w_out)) * share).astype(BF16)
     pre = dot(mixed, w_update)
-    updated = (states + silu(pre)).astype(BF16)
     grad_pre = (cotangent * silu_grad(pre)).astype(BF16)
     grad_sum = (dot(grad_pre, w_update, NT) * share).astype(BF16)
     grad_hidden = dot(grad_sum, w_out, NT).astype(BF16)
-    return updated, mixed, grad_pre, high, low, grad_sum, grad_hidden
+    return mixed, pre, grad_pre, high, low, grad_sum, grad_hidden
+
+
+def state_body(mixed_ref, w_up_ref, far_ref, new_ref, state_ref, sem):
+    copy = pltpu.make_async_copy(far_ref, state_ref, sem)
+    copy.start()
+    change = silu(dot(mixed_ref[...], w_up_ref[...]))
+    copy.wait()
+    new_ref[...] = (state_ref[...].astype(F32) + change).astype(BF16)
 
 
 def master_body(lay, n_far, near_ref, wide_ref, back_ref, *refs):
     far, refs = refs[:n_far], refs[n_far:]
-    new_ref, mixed_ref, pre_ref, high_ref, low_ref, sum_ref, out_ref = refs[:7]
-    near, sems = list(refs[-3:-1]) + list(refs[7:-3]), refs[-1]
+    mixed_ref, pre_ref, high_ref, low_ref, sum_ref, out_ref = refs[:6]
+    near, sems = list(refs[-3:-1]) + list(refs[6:-3]), refs[-1]
     copies = [pltpu.make_async_copy(a, b, sems.at[i]) for i, (a, b) in enumerate(zip(far, near))]
     for copy in copies:
         copy.start()
@@ -208,10 +215,9 @@
         w_out_ref[...],
         w_up_ref[...],
     )
-    updated, mixed, grad_pre, high, low, grad_sum, grad_hidden = results
+    mixed, _, grad_pre, high, low, grad_sum, grad_hidden = results
     select = (iota((rows, lay.rows), 0) == near_ref[...]).astype(BF16)
     out_ref[...] = dot(select, grad_hidden, TN)
-    new_ref[...] = updated
     mixed_ref[...] = mixed
     pre_ref[...] = grad_pre
     high_ref[...] = high
@@ -231,16 +237,17 @@
     for part in parts[1:]:
         total += part[...]
     width = rows_ref.shape[1]
+    states = state_ref[...].astype(F32)
     results = update_rows(
-        state_ref[...].astype(F32),
+        states,
         cot_ref[...].astype(F32),
         total[:, :width],
         total[:, width : width + 1],
         w_out_ref[...],
         w_up_ref[...],
     )
-    updated, mixed, grad_pre, high, low, grad_sum, grad_hidden = results
-    new_ref[...] = updated
+    mixed, pre, grad_pre, high, low, grad_sum, grad_hidden = results
+    new_ref[...] = (states + silu(pre)).astype(BF16)
     mixed_ref[...] = mixed
     pre_ref[...] = grad_pre
     high_ref[...] = high
@@ -525,7 +532,6 @@
         return [
             ((count, width), BF16),
             ((count, width), BF16),
-            ((count, width), BF16),
             ((count, hid), BF16),
             ((count, hid), BF16),
             ((count, width), BF16),
@@ -544,11 +550,11 @@
         flops=2 * rows * (2 * lay.rows * hid + 2 * width * width + 2 * width * hid),
         far=len(far),
     )
-    new_state, saved, grad_rows = master[0], list(master[1:6]), master[6]
-    w_out, w_up, hub_rows, hub_grads = master[7:]
+    saved, grad_rows = list(master[:5]), master[5]
+    w_out, w_up, hub_rows, hub_grads = master[6:]
     new_hub, *hub_saved, grad_message = run(
         body(hub_body, lay, n_group),
-        row_outs(hubs) + [((lay.rows, hid), BF16)],
+        [((hubs, width), BF16)] + row_outs(hubs) + [((lay.rows, hid), BF16)],
         parts + [hub_rows, hub_grads, w_out, w_up, grad_rows],
     )
     grad_table = lax.all_to_all(grad_message, "dev", 0, 0, tiled=True)
@@ -594,8 +600,16 @@
         whole = run(settle_body, [((block, width), BF16)], [own, *terms])
     else:
         whole = total(own, terms).astype(BF16)
-    for cube in (line, flat):
-        whole = cube.gather(whole)
+    new_state = run(
+        state_body,
+        [((rows, width), BF16)],
+        [saved[0], w_up, node_state],
+        scratch=[pltpu.VMEM((rows, width), BF16), pltpu.SemaphoreType.DMA],
+        flops=2 * rows * width * width,
+        far=1,
+    )
+    whole, new_state = lax.optimization_barrier((line.gather(whole), new_state))
+    whole = flat.gather(whole)
     if depths[1] % 8 == 0:
         grad_update, grad_out, grad_in = run(
             body(finish_body, n_group * n_dev // 2),

time: 91 us -> 90.5 us (level)
  waiting for transfers between devices: 35.3 us -> 32.1 us
  Pallas kernels: 19 us -> 20.8 us
  local copies, waits for them, and re-layouts: 2.28 us -> 3.22 us
    ppermute x18, waiting for transfers between devices: 17.8 us -> 15.5 us  [send(): return lax.ppermute(value, ('group', 'dev'), pairs)]
    pallas_call x13 -> x14, Pallas kernels: 19 us -> 20.8 us  [call(): pl.pallas_call(body, out_shape=outs[0] if single else outs, in_specs=spec...]
    all_to_all x1, waiting for transfers between devices: 5.44 us -> 4.5 us  [shards(): grad_table = lax.all_to_all(grad_message, 'dev', 0, 0, tiled=True)]
    unnamed x18 -> x22, local copies, waits for them, and re-layouts: 2.28 us -> 3.22 us
  transfers between devices with their start and end apart: 21 -> 21, of which waited for: 14 -> 13; matrix products, arithmetic and copies ran while one was open for 0% -> 0% of each run, Pallas kernels for 14% -> 16%
where the time goes in v4:
time: 90.5 us; the launch traced here: 89.9 us
  starting transfers between devices  32.7 us (36%)
  waiting for transfers between devices  32.1 us (35%)
  Pallas kernels  20.8 us (23%)
  local copies, waits for them, and re-layouts  3.22 us (4%)
    pallas_call x14, Pallas kernels, call(): pl.pallas_call(body, out_shape=outs[0] if single else outs, in_specs=spec...  20.8 us
    ppermute x18, starting transfers between devices, send(): return lax.ppermute(value, ('group', 'dev'), pairs)  18.4 us
    ppermute x18, waiting for transfers between devices, send(): return lax.ppermute(value, ('group', 'dev'), pairs)  15.5 us
    all_to_all x1, waiting for transfers between devices, shards(): table = lax.all_to_all(packed, 'dev', 0, 0, tiled=True)  7.4 us
    all_to_all x1, starting transfers between devices, shards(): table = lax.all_to_all(packed, 'dev', 0, 0, tiled=True)  7.4 us
    all_to_all x1, waiting for transfers between devices, shards(): back = lax.all_to_all(message, 'dev', 0, 0, tiled=True)  4.63 us
    all_to_all x1, waiting for transfers between devices, shards(): grad_table = lax.all_to_all(grad_message, 'dev', 0, 0, tiled=True)  4.5 us
    all_to_all x1, starting transfers between devices, shards(): back = lax.all_to_all(message, 'dev', 0, 0, tiled=True)  3.59 us
  transfers between devices with their start and end apart: 21, of which 13 were waited for; matrix products, arithmetic and copies ran while one was open for 0% of the time, Pallas kernels for 16%

profile of v4, /device:TPU:0, one launch (start us, length us, event | category | flops | bytes accessed | tf_op | source)
XLA Modules:
  0.0 89.9 jit_solution(15433127830510141213)
XLA Ops:
  0.6 2.3 %shard_map.156 = bf16[320,512]{1,0:T(8,128)(2,1)} custom-call(s32[1,8]{1,0:T(1,128)} %count_ref.3, s32[8,32]{1,0:T(8,128)} %bitcast.16, bf16[512,512]{1,0:T(8,128)(2,1)} %far_ref.1, bf16[8,512]{1,0:T(8,128)(2,1)} %refs_4_.1), custom_call_target="tpu_custom_call" | custom-call | bytes 861216 | tf_op jit(solution)/shard_map/pallas_call | solution.py:382
  2.9 7.4 %all-to-all-start = ((bf16[8,40,512]{2,1,0:T(8,128)(2,1)}), bf16[8,40,512]{2,1,0:T(8,128)(2,1)S(1)}, u32[]{:S(2)}, u32[]{:S(2)}) async-start(bf16[8,40,512]{2,1,0:T(8,128)(2,1)} %bitcast.18), calls=%async_computation | async-start | bytes 655360 | tf_op jit(solution)/shard_map/all_to_all | solution.py:495
  10.4 2.9 %shard_map.155 = (bf16[320,320]{1,0:T(8,128)(2,1)S(1)}, bf16[320,320]{1,0:T(8,128)(2,1)S(1)}, bf16[384,256]{1,0:T(8,128)(2,1)S(1)}, s32[1,320]{1,0:T(1,128)S(1)}, s32[1,384]{1,0:T(1,128)S(1)}) custom-call(s32[1,8]{1,0:T(1,128)S(1)} %copy-done.7, s32[8,32]{1,0:T(8,128)S(1)} %bitcast.17, s32[4096]{0:T(1024)S(1)} %copy-done.8, s32[4096]{0:T(1024)S(1)} %copy-done.9, ...), custom_call_target="tpu_custom_call" | custom-call | flops 838860800 | bytes 659232 | tf_op jit(solution)/shard_map/pallas_call | solution.py:382
  13.3 7.4 %all-to-all-done = bf16[8,40,512]{2,1,0:T(8,128)(2,1)S(1)} async-done(((bf16[8,40,512]{2,1,0:T(8,128)(2,1)}), bf16[8,40,512]{2,1,0:T(8,128)(2,1)S(1)}, u32[]{:S(2)}, u32[]{:S(2)}) %all-to-all-start) | async-done | bytes 327712 | tf_op jit(solution)/shard_map/all_to_all | solution.py:495
  21.9 3.6 %all-to-all-start.1 = ((bf16[8,48,256]{2,1,0:T(8,128)(2,1)}), bf16[8,48,256]{2,1,0:T(8,128)(2,1)S(1)}, u32[]{:S(2)}, u32[]{:S(2)}) async-start(bf16[8,48,256]{2,1,0:T(8,128)(2,1)} %bitcast.7), calls=%async_computation.1 | async-start | bytes 393216 | tf_op jit(solution)/shard_map/all_to_all | solution.py:518
  28.6 4.6 %all-to-all-done.1 = bf16[8,48,256]{2,1,0:T(8,128)(2,1)S(1)} async-done(((bf16[8,48,256]{2,1,0:T(8,128)(2,1)}), bf16[8,48,256]{2,1,0:T(8,128)(2,1)S(1)}, u32[]{:S(2)}, u32[]{:S(2)}) %all-to-all-start.1) | async-done | bytes 196640 | tf_op jit(solution)/shard_map/all_to_all | solution.py:518
  33.4 1.6 %collective-permute-start.1 = (f32[8,384]{1,0:T(8,128)S(1)}, f32[8,384]{1,0:T(8,128)S(1)}, u32[]{:S(2)}, u32[]{:S(2)}) collective-permute-start(f32[8,384]{1,0:T(8,128)S(1)} %shard_map.160.refs_0_), channel_id=1, source_target_pairs={{0,16},{1,17},{2,18},{3,19},{4,20},{5,21},{6,22},{7,23},{8,24},{9,... | collective-permute-start | bytes 36872 | tf_op jit(solution)/shard_map/ppermute | solution.py:411
  35.2 3.6 %shard_map.159 = (bf16[512,512]{1,0:T(8,128)(2,1)S(1)}, bf16[512,512]{1,0:T(8,128)(2,1)S(1)}, bf16[512,256]{1,0:T(8,128)(2,1)S(1)}, bf16[512,256]{1,0:T(8,128)(2...) custom-call(s32[1,320]{1,0:T(1,128)S(1)} %get-tuple-element.51.near_, ...), custom_call_target="tpu_custom_call" | custom-call | flops 973078528 | bytes 5278464 | tf_op jit(solution)/shard_map/pallas_call | solution.py:382
  40.3 3.4 %all-to-all-start.2 = ((bf16[8,40,256]{2,1,0:T(8,128)(2,1)}), bf16[8,40,256]{2,1,0:T(8,128)(2,1)S(1)}, u32[]{:S(2)}, u32[]{:S(2)}) async-start(bf16[8,40,256]{2,1,0:T(8,128)(2,1)} %bitcast.9), calls=%async_computation.2 | async-start | bytes 327680 | tf_op jit(solution)/shard_map/all_to_all | solution.py:560
  44.6 2.4 %shard_map.162 = (f32[384,512]{1,0:T(8,128)S(1)}, bf16[384,512]{1,0:T(8,128)(2,1)}) custom-call(s32[2]{0:T(128)S(1)} %pad_add_fusion.place_ref, bf16[512,512]{1,0:T(8,128)(2,1)S(1)} %get-tuple-element.60.mixed_ref, bf16[512,512]{1,0:T(8,128)(2,1)S(1)} %get-tuple-element.61.pre_ref, bf16[512,256]{1,0:T(8,128)(2,1)S(1)} %get-tuple-element.62.high_ref, ...), custom_call_target="tpu_custom_call" | custom-call | flops 536870912 | bytes 3309576 | tf_op jit(solution)/shard_map/pallas_call | solution.py:382
  47.4 4.5 %all-to-all-done.2 = bf16[8,40,256]{2,1,0:T(8,128)(2,1)S(1)} async-done(((bf16[8,40,256]{2,1,0:T(8,128)(2,1)}), bf16[8,40,256]{2,1,0:T(8,128)(2,1)S(1)}, u32[]{:S(2)}, u32[]{:S(2)}) %all-to-all-start.2) | async-done | bytes 163872 | tf_op jit(solution)/shard_map/all_to_all | solution.py:560
  51.9 2.3 %shard_map.163 = (f32[128,512]{1,0:T(8,128)S(1)}, bf16[128,512]{1,0:T(8,128)(2,1)S(1)}) custom-call(s32[1]{0:T(128)} %bitcast.3.place_ref, bf16[320,256]{1,0:T(8,128)(2,1)S(1)} %bitcast.15, bf16[640,320]{1,0:T(8,128)(2,1)} %copy-done.1, f32[320,256]{1,0:T(8,128)} %copy-done.3, bf16[512,320]{1,0:T(8,128)(2,1)} %copy-done.2), custom_call_target="tpu_custom_call" | custom-call | flops 272629760 | bytes 1622020 | tf_op jit(solution)/shard_map/pallas_call | solution.py:382
  56.1 1.5 %collective-permute-start.6 = (bf16[128,512]{1,0:T(8,128)(2,1)S(1)}, bf16[128,512]{1,0:T(8,128)(2,1)S(1)}, u32[]{:S(2)}, u32[]{:S(2)}) collective-permute-start(bf16[128,512]{1,0:T(8,128)(2,1)S(1)} %get-tuple-element.85), channel_id=1, source_target_pairs={{0,16},{1,17},{2,18},{3,19},{4,20},{5,21},{6,22},{7,23},{8,24},{9,... | collective-permute-start | bytes 393224 | tf_op jit(solution)/shard_map/ppermute | solution.py:411
  57.6 1.7 %collective-permute-start.7 = (bf16[128,512]{1,0:T(8,128)(2,1)S(1)}, bf16[128,512]{1,0:T(8,128)(2,1)S(1)}, u32[]{:S(2)}, u32[]{:S(2)}) collective-permute-start(bf16[128,512]{1,0:T(8,128)(2,1)S(1)} %get-tuple-element.86), channel_id=1, source_target_pairs={{0,17},{1,16},{2,19},{3,18},{4,21},{5,20},{6,23},{7,22},{8,25},{9,... | collective-permute-start | bytes 393224 | tf_op jit(solution)/shard_map/ppermute | solution.py:411
  59.3 2.9 %collective-permute-done.5.refs_1_ = bf16[128,512]{1,0:T(8,128)(2,1)S(1)} collective-permute-done((bf16[128,512]{1,0:T(8,128)(2,1)S(1)}, bf16[128,512]{1,0:T(8,128)(2,1)S(1)}, u32[]{:S(2)}, u32[]{:S(2)}) %collective-permute-start.5) | collective-permute-done | bytes 131104 | tf_op jit(solution)/shard_map/ppermute | solution.py:411
  62.1 3.0 %collective-permute-done.7.refs_3_ = bf16[128,512]{1,0:T(8,128)(2,1)S(1)} collective-permute-done((bf16[128,512]{1,0:T(8,128)(2,1)S(1)}, bf16[128,512]{1,0:T(8,128)(2,1)S(1)}, u32[]{:S(2)}, u32[]{:S(2)}) %collective-permute-start.7) | collective-permute-done | bytes 131104 | tf_op jit(solution)/shard_map/ppermute | solution.py:411
  66.3 3.3 %collective-permute-start.9 = (bf16[32,512]{1,0:T(8,128)(2,1)S(1)}, bf16[32,512]{1,0:T(8,128)(2,1)S(1)}, u32[]{:S(2)}, u32[]{:S(2)}) collective-permute-start(bf16[32,512]{1,0:T(8,128)(2,1)S(1)} %get-tuple-element.89), channel_id=1, source_target_pairs={{0,4},{1,5},{2,6},{3,7},{4,0},{5,1},{6,2},{7,3},{8,12},{9,13},{10,... | collective-permute-start | bytes 98312 | tf_op jit(solution)/shard_map/ppermute | solution.py:411
  71.6 2.4 %collective-permute-start.11 = (bf16[32,512]{1,0:T(8,128)(2,1)S(1)}, bf16[32,512]{1,0:T(8,128)(2,1)S(1)}, u32[]{:S(2)}, u32[]{:S(2)}) collective-permute-start(bf16[32,512]{1,0:T(8,128)(2,1)S(1)} %shard_map.166), channel_id=1, source_target_pairs={{0,6},{1,7},{2,4},{3,5},{4,2},{5,3},{6,0},{7,1},{8,14},{9,15},{10,... | collective-permute-start | bytes 98312 | tf_op jit(solution)/shard_map/ppermute | solution.py:411
  74.6 1.4 %collective-permute-start.13 = (bf16[32,512]{1,0:T(8,128)(2,1)S(1)}, bf16[32,512]{1,0:T(8,128)(2,1)S(1)}, u32[]{:S(2)}, u32[]{:S(2)}) collective-permute-start(bf16[32,512]{1,0:T(8,128)(2,1)S(1)} %shard_map.166), channel_id=1, source_target_pairs={{0,2},{1,3},{2,0},{3,1},{4,6},{5,7},{6,4},{7,5},{8,10},{9,11},{10,... | collective-permute-start | bytes 98312 | tf_op jit(solution)/shard_map/ppermute | solution.py:411
  76.0 2.2 %shard_map.167 = bf16[512,512]{1,0:T(8,128)(2,1)} custom-call(bf16[512,512]{1,0:T(8,128)(2,1)S(1)} %get-tuple-element.60.mixed_ref, bf16[512,512]{1,0:T(8,128)(2,1)S(1)} %get-tuple-element.68.refs_7_.w_up_ref, bf16[512,512]{1,0:T(8,128)(2,1)} %far_ref.1), custom_call_target="tpu_custom_call" | custom-call | flops 268435456 | bytes 2097152 | tf_op jit(solution)/shard_map/pallas_call | solution.py:382
  78.9 1.8 %collective-permute-start.14 = (bf16[128,512]{1,0:T(8,128)(2,1)S(1)}, bf16[128,512]{1,0:T(8,128)(2,1)S(1)}, u32[]{:S(2)}, u32[]{:S(2)}) collective-permute-start(bf16[128,512]{1,0:T(8,128)(2,1)S(1)} %pad_maximum_fusion.1), channel_id=1, source_target_pairs={{0,17},{1,16},{2,19},{3,18},{4,21},{5,20},{6,23},{7,22},{8,25},{9,... | collective-permute-start | bytes 393224 | tf_op jit(solution)/shard_map/ppermute | solution.py:411
  82.5 2.4 %collective-permute-done.14 = bf16[128,512]{1,0:T(8,128)(2,1)S(1)} collective-permute-done((bf16[128,512]{1,0:T(8,128)(2,1)S(1)}, bf16[128,512]{1,0:T(8,128)(2,1)S(1)}, u32[]{:S(2)}, u32[]{:S(2)}) %collective-permute-start.14) | collective-permute-done | bytes 131104 | tf_op jit(solution)/shard_map/ppermute | solution.py:411
  86.7 1.9 %collective-permute-done.17.other_ref = bf16[512,512]{1,0:T(8,128)(2,1)S(1)} collective-permute-done((bf16[512,512]{1,0:T(8,128)(2,1)S(1)}, bf16[512,512]{1,0:T(8,128)(2,1)S(1)}, u32[]{:S(2)}, u32[]{:S(2)}) %collective-permute-start.17) | collective-permute-done | bytes 524320 | tf_op jit(solution)/shard_map/ppermute | solution.py:411
  88.6 1.4 %shard_map.168 = (f32[512,512]{1,0:T(8,128)}, f32[256,512]{1,0:T(8,128)}, f32[512,256]{1,0:T(8,128)}) custom-call(s32[1]{0:T(128)} %bitcast.3.place_ref, bf16[512,512]{1,0:T(8,128)(2,1)S(1)} %pad_maximum_fusion.own_ref, bf16[512,512]{1,0:T(8,128)(2,1)S(1)} %collective-permute-done.17.other_ref), custom_call_target="tpu_custom_call" | custom-call | bytes 3145732 | tf_op jit(solution)/shard_map/pallas_call | solution.py:382
  (59 shorter events, 17.3 us)
Async XLA Ops:
  2.9 7.4 %copy-start.9 = (s32[4096]{0:T(1024)S(1)}, s32[4096]{0:T(1024)}, u32[]{:S(2)}) copy-start(s32[4096]{0:T(1024)} %dst_ref.1) | copy-start | bytes 49156
  2.9 7.4 %copy-start.10 = (s32[4096]{0:T(1024)S(1)}, s32[4096]{0:T(1024)}, u32[]{:S(2)}) copy-start(s32[4096]{0:T(1024)} %mask_ref.1) | copy-start | bytes 49156
  2.9 17.7 %all-to-all-start = ((bf16[8,40,512]{2,1,0:T(8,128)(2,1)}), bf16[8,40,512]{2,1,0:T(8,128)(2,1)S(1)}, u32[]{:S(2)}, u32[]{:S(2)}) async-start(bf16[8,40,512]{2,1,0:T(8,128)(2,1)} %bitcast.18), calls=%async_computation | async-start | bytes 655360 | tf_op jit(solution)/shard_map/all_to_all | solution.py:495
  10.4 10.3 %copy-start = (bf16[512,256]{1,0:T(8,128)(2,1)S(1)}, bf16[512,256]{1,0:T(8,128)(2,1)}, u32[]{:S(2)}) copy-start(bf16[512,256]{1,0:T(8,128)(2,1)} %w_ref.3) | copy-start | bytes 786436
  21.9 11.4 %all-to-all-start.1 = ((bf16[8,48,256]{2,1,0:T(8,128)(2,1)}), bf16[8,48,256]{2,1,0:T(8,128)(2,1)S(1)}, u32[]{:S(2)}, u32[]{:S(2)}) async-start(bf16[8,48,256]{2,1,0:T(8,128)(2,1)} %bitcast.7), calls=%async_computation.1 | async-start | bytes 393216 | tf_op jit(solution)/shard_map/all_to_all | solution.py:518
  33.4 5.5 %collective-permute-start = (f32[8,384]{1,0:T(8,128)S(1)}, f32[8,384]{1,0:T(8,128)S(1)}, u32[]{:S(2)}, u32[]{:S(2)}) collective-permute-start(f32[8,384]{1,0:T(8,128)S(1)} %shard_map.160.refs_0_), channel_id=1, source_target_pairs={{0,8},{1,9},{2,10},{3,11},{4,12},{5,13},{6,14},{7,15},{8,0},{9,1},... | collective-permute-start | bytes 36872 | tf_op jit(solution)/shard_map/ppermute | solution.py:411
  33.4 5.5 %collective-permute-start.1 = (f32[8,384]{1,0:T(8,128)S(1)}, f32[8,384]{1,0:T(8,128)S(1)}, u32[]{:S(2)}, u32[]{:S(2)}) collective-permute-start(f32[8,384]{1,0:T(8,128)S(1)} %shard_map.160.refs_0_), channel_id=1, source_target_pairs={{0,16},{1,17},{2,18},{3,19},{4,20},{5,21},{6,22},{7,23},{8,24},{9,... | collective-permute-start | bytes 36872 | tf_op jit(solution)/shard_map/ppermute | solution.py:411
  35.0 3.9 %collective-permute-start.2 = (f32[8,384]{1,0:T(8,128)S(1)}, f32[8,384]{1,0:T(8,128)S(1)}, u32[]{:S(2)}, u32[]{:S(2)}) collective-permute-start(f32[8,384]{1,0:T(8,128)S(1)} %shard_map.160.refs_0_), channel_id=1, source_target_pairs={{0,24},{1,25},{2,26},{3,27},{4,28},{5,29},{6,30},{7,31},{8,16},{9,... | collective-permute-start | bytes 36872 | tf_op jit(solution)/shard_map/ppermute | solution.py:411
  40.3 11.6 %all-to-all-start.2 = ((bf16[8,40,256]{2,1,0:T(8,128)(2,1)}), bf16[8,40,256]{2,1,0:T(8,128)(2,1)S(1)}, u32[]{:S(2)}, u32[]{:S(2)}) async-start(bf16[8,40,256]{2,1,0:T(8,128)(2,1)} %bitcast.9), calls=%async_computation.2 | async-start | bytes 327680 | tf_op jit(solution)/shard_map/all_to_all | solution.py:560
  47.0 7.2 %collective-permute-start.3 = (bf16[384,512]{1,0:T(8,128)(2,1)}, bf16[384,512]{1,0:T(8,128)(2,1)S(1)}, u32[]{:S(2)}, u32[]{:S(2)}) collective-permute-start(bf16[384,512]{1,0:T(8,128)(2,1)} %get-tuple-element.76), channel_id=1, source_target_pairs={{0,8},{1,9},{2,10},{3,11},{4,12},{5,13},{6,14},{7,15},{8,0},{9,1},... | collective-permute-start | bytes 1179656 | tf_op jit(solution)/shard_map/ppermute | solution.py:411
  54.1 1.4 %collective-permute-start.4 = (bf16[128,512]{1,0:T(8,128)(2,1)S(1)}, bf16[128,512]{1,0:T(8,128)(2,1)S(1)}, u32[]{:S(2)}, u32[]{:S(2)}) collective-permute-start(bf16[128,512]{1,0:T(8,128)(2,1)S(1)} %get-tuple-element.82), channel_id=1, source_target_pairs={{0,8},{1,9},{2,10},{3,11},{4,12},{5,13},{6,14},{7,15},{8,0},{9,1},... | collective-permute-start | bytes 393224 | tf_op jit(solution)/shard_map/ppermute | solution.py:411
  55.7 6.4 %collective-permute-start.5 = (bf16[128,512]{1,0:T(8,128)(2,1)S(1)}, bf16[128,512]{1,0:T(8,128)(2,1)S(1)}, u32[]{:S(2)}, u32[]{:S(2)}) collective-permute-start(bf16[128,512]{1,0:T(8,128)(2,1)S(1)} %get-tuple-element.84), channel_id=1, source_target_pairs={{0,1},{1,0},{2,3},{3,2},{4,5},{5,4},{6,7},{7,6},{8,9},{9,8},{10,11... | collective-permute-start | bytes 393224 | tf_op jit(solution)/shard_map/ppermute | solution.py:411
  56.1 6.0 %collective-permute-start.6 = (bf16[128,512]{1,0:T(8,128)(2,1)S(1)}, bf16[128,512]{1,0:T(8,128)(2,1)S(1)}, u32[]{:S(2)}, u32[]{:S(2)}) collective-permute-start(bf16[128,512]{1,0:T(8,128)(2,1)S(1)} %get-tuple-element.85), channel_id=1, source_target_pairs={{0,16},{1,17},{2,18},{3,19},{4,20},{5,21},{6,22},{7,23},{8,24},{9,... | collective-permute-start | bytes 393224 | tf_op jit(solution)/shard_map/ppermute | solution.py:411
  57.6 7.5 %collective-permute-start.7 = (bf16[128,512]{1,0:T(8,128)(2,1)S(1)}, bf16[128,512]{1,0:T(8,128)(2,1)S(1)}, u32[]{:S(2)}, u32[]{:S(2)}) collective-permute-start(bf16[128,512]{1,0:T(8,128)(2,1)S(1)} %get-tuple-element.86), channel_id=1, source_target_pairs={{0,17},{1,16},{2,19},{3,18},{4,21},{5,20},{6,23},{7,22},{8,25},{9,... | collective-permute-start | bytes 393224 | tf_op jit(solution)/shard_map/ppermute | solution.py:411
  65.2 5.8 %collective-permute-start.10 = (bf16[32,512]{1,0:T(8,128)(2,1)S(1)}, bf16[32,512]{1,0:T(8,128)(2,1)S(1)}, u32[]{:S(2)}, u32[]{:S(2)}) collective-permute-start(bf16[32,512]{1,0:T(8,128)(2,1)S(1)} %get-tuple-element.90), channel_id=1, source_target_pairs={{0,6},{1,7},{2,4},{3,5},{4,2},{5,3},{6,0},{7,1},{8,14},{9,15},{10,... | collective-permute-start | bytes 98312 | tf_op jit(solution)/shard_map/ppermute | solution.py:411
  66.2 4.8 %collective-permute-start.8 = (bf16[32,512]{1,0:T(8,128)(2,1)S(1)}, bf16[32,512]{1,0:T(8,128)(2,1)S(1)}, u32[]{:S(2)}, u32[]{:S(2)}) collective-permute-start(bf16[32,512]{1,0:T(8,128)(2,1)S(1)} %get-tuple-element.88), channel_id=1, source_target_pairs={{0,2},{1,3},{2,0},{3,1},{4,6},{5,7},{6,4},{7,5},{8,10},{9,11},{10,... | collective-permute-start | bytes 98312 | tf_op jit(solution)/shard_map/ppermute | solution.py:411
  66.3 5.2 %collective-permute-start.9 = (bf16[32,512]{1,0:T(8,128)(2,1)S(1)}, bf16[32,512]{1,0:T(8,128)(2,1)S(1)}, u32[]{:S(2)}, u32[]{:S(2)}) collective-permute-start(bf16[32,512]{1,0:T(8,128)(2,1)S(1)} %get-tuple-element.89), channel_id=1, source_target_pairs={{0,4},{1,5},{2,6},{3,7},{4,0},{5,1},{6,2},{7,3},{8,12},{9,13},{10,... | collective-permute-start | bytes 98312 | tf_op jit(solution)/shard_map/ppermute | solution.py:411
  71.6 6.7 %collective-permute-start.11 = (bf16[32,512]{1,0:T(8,128)(2,1)S(1)}, bf16[32,512]{1,0:T(8,128)(2,1)S(1)}, u32[]{:S(2)}, u32[]{:S(2)}) collective-permute-start(bf16[32,512]{1,0:T(8,128)(2,1)S(1)} %shard_map.166), channel_id=1, source_target_pairs={{0,6},{1,7},{2,4},{3,5},{4,2},{5,3},{6,0},{7,1},{8,14},{9,15},{10,... | collective-permute-start | bytes 98312 | tf_op jit(solution)/shard_map/ppermute | solution.py:411
  74.0 4.9 %collective-permute-start.12 = (bf16[32,512]{1,0:T(8,128)(2,1)S(1)}, bf16[32,512]{1,0:T(8,128)(2,1)S(1)}, u32[]{:S(2)}, u32[]{:S(2)}) collective-permute-start(bf16[32,512]{1,0:T(8,128)(2,1)S(1)} %shard_map.166), channel_id=1, source_target_pairs={{0,4},{1,5},{2,6},{3,7},{4,0},{5,1},{6,2},{7,3},{8,12},{9,13},{10,... | collective-permute-start | bytes 98312 | tf_op jit(solution)/shard_map/ppermute | solution.py:411
  74.6 4.3 %collective-permute-start.13 = (bf16[32,512]{1,0:T(8,128)(2,1)S(1)}, bf16[32,512]{1,0:T(8,128)(2,1)S(1)}, u32[]{:S(2)}, u32[]{:S(2)}) collective-permute-start(bf16[32,512]{1,0:T(8,128)(2,1)S(1)} %shard_map.166), channel_id=1, source_target_pairs={{0,2},{1,3},{2,0},{3,1},{4,6},{5,7},{6,4},{7,5},{8,10},{9,11},{10,... | collective-permute-start | bytes 98312 | tf_op jit(solution)/shard_map/ppermute | solution.py:411
  78.9 6.0 %collective-permute-start.14 = (bf16[128,512]{1,0:T(8,128)(2,1)S(1)}, bf16[128,512]{1,0:T(8,128)(2,1)S(1)}, u32[]{:S(2)}, u32[]{:S(2)}) collective-permute-start(bf16[128,512]{1,0:T(8,128)(2,1)S(1)} %pad_maximum_fusion.1), channel_id=1, source_target_pairs={{0,17},{1,16},{2,19},{3,18},{4,21},{5,20},{6,23},{7,22},{8,25},{9,... | collective-permute-start | bytes 393224 | tf_op jit(solution)/shard_map/ppermute | solution.py:411
  80.7 5.5 %collective-permute-start.15 = (bf16[128,512]{1,0:T(8,128)(2,1)S(1)}, bf16[128,512]{1,0:T(8,128)(2,1)S(1)}, u32[]{:S(2)}, u32[]{:S(2)}) collective-permute-start(bf16[128,512]{1,0:T(8,128)(2,1)S(1)} %pad_maximum_fusion.1), channel_id=1, source_target_pairs={{0,16},{1,17},{2,18},{3,19},{4,20},{5,21},{6,22},{7,23},{8,24},{9,... | collective-permute-start | bytes 393224 | tf_op jit(solution)/shard_map/ppermute | solution.py:411
  81.5 5.0 %collective-permute-start.16 = (bf16[128,512]{1,0:T(8,128)(2,1)S(1)}, bf16[128,512]{1,0:T(8,128)(2,1)S(1)}, u32[]{:S(2)}, u32[]{:S(2)}) collective-permute-start(bf16[128,512]{1,0:T(8,128)(2,1)S(1)} %pad_maximum_fusion.1), channel_id=1, source_target_pairs={{0,1},{1,0},{2,3},{3,2},{4,5},{5,4},{6,7},{7,6},{8,9},{9,8},{10,11... | collective-permute-start | bytes 393224 | tf_op jit(solution)/shard_map/ppermute | solution.py:411
  86.6 2.0 %collective-permute-start.17 = (bf16[512,512]{1,0:T(8,128)(2,1)S(1)}, bf16[512,512]{1,0:T(8,128)(2,1)S(1)}, u32[]{:S(2)}, u32[]{:S(2)}) collective-permute-start(bf16[512,512]{1,0:T(8,128)(2,1)S(1)} %pad_maximum_fusion.own_ref), channel_id=1, source_target_pairs={{0,8},{1,9},{2,10},{3,11},{4,12},{5,13},{6,14},{7,15},{8,0},{9,1},... | collective-permute-start | bytes 1572872 | tf_op jit(solution)/shard_map/ppermute | solution.py:411
  (8 other events, 26.9 us)
